TPU v7x, 32 devices: a whole 2x2x4 slice. The times are simulated.
32 devices in a mesh: dp: 8 (over z, y), fsdp: 4 (over x, core).
Axes of the slice: x: 2, y: 2, z: 4, core: 2. Of those that a mesh axis runs over, the one named last changes fastest.
Arguments:
- inputs: bfloat16 [65536, 384], P(('dp', 'fsdp')), may hold values from -6 to 6
- cotangent: bfloat16 [65536, 384], P(('dp', 'fsdp')), may hold values from -6 to 6
- attn_masks: int32 [1024, 64, 64], P(('dp', 'fsdp')), may hold values 0 or 1
- qkv_weight: float32 [384, 1152], P(('dp', 'fsdp')), may hold values from -0.3125 to 0.3125
- qkv_first: float32 [384, 1152], P(('dp', 'fsdp')), may hold values from -0.0012207031 to 0.0012207031
- qkv_second: float32 [384, 1152], P(('dp', 'fsdp')), may hold values from 2.8257016e-10 to 4.5211226e-09
- proj_weight: float32 [384, 384], P(('dp', 'fsdp')), may hold values from -1.5 to 1.5
- proj_first: float32 [384, 384], P(('dp', 'fsdp')), may hold values from -0.0012207031 to 0.0012207031
- proj_second: float32 [384, 384], P(('dp', 'fsdp')), may hold values from 2.8257016e-10 to 4.5211226e-09
- up_weight: float32 [384, 1536], P(('dp', 'fsdp')), may hold values from -0.3125 to 0.3125
- up_first: float32 [384, 1536], P(('dp', 'fsdp')), may hold values from -0.0012207031 to 0.0012207031
- up_second: float32 [384, 1536], P(('dp', 'fsdp')), may hold values from 2.8257016e-10 to 4.5211226e-09
- down_weight: float32 [1536, 384], P(('dp', 'fsdp')), may hold values from -0.15625 to 0.15625
- down_first: float32 [1536, 384], P(('dp', 'fsdp')), may hold values from -0.0012207031 to 0.0012207031
- down_second: float32 [1536, 384], P(('dp', 'fsdp')), may hold values from 2.8257016e-10 to 4.5211226e-09
- vectors: float32 [3840], P(('dp', 'fsdp')), may hold values from -1.5 to 4.5, as said below
- vector_first: float32 [3840], P(('dp', 'fsdp')), may hold values from -0.0048828125 to 0.0048828125
- vector_second: float32 [3840], P(('dp', 'fsdp')), may hold values from 4.5211226e-09 to 7.233796e-08
Outputs:
- block_out: bfloat16 [65536, 384], P(('dp', 'fsdp'))
- input_grad: float32 [65536, 384], P(('dp', 'fsdp'))
- clip_norm: float32 [], replicated
- qkv_new: float32 [384, 1152], P(('dp', 'fsdp'))
- qkv_first_new: float32 [384, 1152], P(('dp', 'fsdp'))
- qkv_second_new: float32 [384, 1152], P(('dp', 'fsdp'))
- proj_new: float32 [384, 384], P(('dp', 'fsdp'))
- proj_first_new: float32 [384, 384], P(('dp', 'fsdp'))
- proj_second_new: float32 [384, 384], P(('dp', 'fsdp'))
- up_new: float32 [384, 1536], P(('dp', 'fsdp'))
- up_first_new: float32 [384, 1536], P(('dp', 'fsdp'))
- up_second_new: float32 [384, 1536], P(('dp', 'fsdp'))
- down_new: float32 [1536, 384], P(('dp', 'fsdp'))
- down_first_new: float32 [1536, 384], P(('dp', 'fsdp'))
- down_second_new: float32 [1536, 384], P(('dp', 'fsdp'))
- vector_new: float32 [3840], P(('dp', 'fsdp'))
- vector_first_new: float32 [3840], P(('dp', 'fsdp'))
- vector_second_new: float32 [3840], P(('dp', 'fsdp'))
Inputs may be any that keep to these rules, and one draw needn't show every extreme that they name: `vectors`: gains and biases of a trained layer.
All inputs are finite; a program needn't handle non-finite values. No bound on the sum of `attn_masks` on one device may be relied on, other than what follows from the above.
Results may differ from a plain program's by a relative error of at most 0.008.
The roundings to bfloat16 on the way count: a program that leaves them out, or rounds other values in their place, can miss the bound.
Values may be sent and summed in bfloat16 or wider, within the bound.
A program may use at most 128 MiB of HBM per device.

v0:
```python
import jax
import jax.numpy as jnp
from jax import lax
from jax.sharding import PartitionSpec as P

D = 384
FF = 1536
HEADS = 6
HD = 64
P_SIZE = 64
STEP = 10


norm_eps = 1e-05
beta_first = 0.9
beta_second = 0.999
adam_eps = 1e-08
decay_rate = 0.05
matrix_rates = (0.1, 0.5, 0.1, 0.05)
vector_rate = 1.0


def layer_norm(values, scales, offset):
    average = jnp.mean(values, axis=-1, keepdims=True)
    centered = values - average
    variance = jnp.mean(centered * centered, axis=-1, keepdims=True)
    return centered * lax.rsqrt(variance + norm_eps) * scales + offset


def split_vector(vector):
    return (
        vector[0:D],
        vector[D : 2 * D],
        vector[2 * D : 3 * D],
        vector[3 * D : 4 * D],
        vector[4 * D : 5 * D],
        vector[5 * D : 6 * D],
        vector[6 * D : 6 * D + FF],
    )


def make_allowed(attn_masks):
    query_pos = lax.broadcasted_iota(jnp.int32, (P_SIZE, P_SIZE), 0)
    key_pos = lax.broadcasted_iota(jnp.int32, (P_SIZE, P_SIZE), 1)
    return (key_pos <= query_pos) & ((attn_masks == 1) | (key_pos == query_pos))


def gelu_exact(values):
    return jax.nn.gelu(values, approximate=False)


def masked_scores(queries, keys_part, allowed):
    raw_scores = jnp.einsum(
        "cqhd,ckhd->chqk", queries, keys_part, preferred_element_type=jnp.float32
    ) * HD ** (-0.5)
    return jnp.where(allowed, raw_scores, -1e30)


def adam_step(master, moment_one, moment_two, gradient, step_rate, decay_coef):
    first_new = beta_first * moment_one + (1.0 - beta_first) * gradient
    second_new = beta_second * moment_two + (1.0 - beta_second) * gradient * gradient
    first_hat = first_new / (1.0 - beta_first**STEP)
    second_hat = second_new / (1.0 - beta_second**STEP)
    master_new = master - step_rate * (
        first_hat / (jnp.sqrt(second_hat) + adam_eps) + decay_coef * master
    )
    return (master_new, first_new, second_new)


def per_device(
    inputs,
    cotangent,
    attn_masks,
    qkv_weight,
    qkv_first,
    qkv_second,
    proj_weight,
    proj_first,
    proj_second,
    up_weight,
    up_first,
    up_second,
    down_weight,
    down_first,
    down_second,
    vectors,
    vector_first,
    vector_second,
):
    qkv_low = qkv_weight.astype(jnp.bfloat16)
    proj_low = proj_weight.astype(jnp.bfloat16)
    up_low = up_weight.astype(jnp.bfloat16)
    down_low = down_weight.astype(jnp.bfloat16)
    vector_low = vectors.astype(jnp.bfloat16)
    qkv_full, proj_full, up_full, down_full, vector_full = (
        lax.all_gather(qkv_low, ("dp", "fsdp"), axis=0, tiled=True),
        lax.all_gather(proj_low, ("dp", "fsdp"), axis=0, tiled=True),
        lax.all_gather(up_low, ("dp", "fsdp"), axis=0, tiled=True),
        lax.all_gather(down_low, ("dp", "fsdp"), axis=0, tiled=True),
        lax.all_gather(vector_low, ("dp", "fsdp"), axis=0, tiled=True),
    )
    gain_one, bias_one, gain_two, bias_two, proj_bias, down_bias, up_bias = split_vector(
        vector_full.astype(jnp.float32)
    )
    rows_here = inputs.shape[0]
    clouds_here = rows_here // P_SIZE
    layer_input = inputs.astype(jnp.float32)
    normed_value, norm_one_pull = jax.vjp(layer_norm, layer_input, gain_one, bias_one)
    normed = normed_value.astype(jnp.bfloat16)
    packed = jnp.dot(normed, qkv_full, preferred_element_type=jnp.float32).astype(jnp.bfloat16)
    shaped = packed.reshape(clouds_here, P_SIZE, 3, HEADS, HD)
    queries = shaped[:, :, 0]
    keys_part = shaped[:, :, 1]
    values = shaped[:, :, 2]
    allowed = make_allowed(attn_masks)[:, None]
    scores = masked_scores(queries, keys_part, allowed)
    top_score = jnp.max(scores, axis=-1, keepdims=True)
    exponent = jnp.exp(scores - top_score)
    total = jnp.sum(exponent, axis=-1, keepdims=True)
    log_total = top_score + jnp.log(total)
    weights = (exponent / total).astype(jnp.bfloat16)
    mixture = jnp.einsum("chqk,ckhd->cqhd", weights, values, preferred_element_type=jnp.float32)
    mixture = mixture.reshape(rows_here, D).astype(jnp.bfloat16)
    branch = jnp.dot(mixture, proj_full, preferred_element_type=jnp.float32) + proj_bias
    middle = layer_input + branch
    second_value, norm_two_pull = jax.vjp(layer_norm, middle, gain_two, bias_two)
    second = second_value.astype(jnp.bfloat16)
    hidden = jnp.dot(second, up_full, preferred_element_type=jnp.float32) + up_bias
    active_value, gelu_pull = jax.vjp(gelu_exact, hidden)
    active = active_value.astype(jnp.bfloat16)
    branch_two = jnp.dot(active, down_full, preferred_element_type=jnp.float32) + down_bias
    block_out = (middle + branch_two).astype(jnp.bfloat16)
    qkv_back, proj_back, up_back, down_back = (
        lax.all_gather(qkv_low, ("dp", "fsdp"), axis=0, tiled=True),
        lax.all_gather(proj_low, ("dp", "fsdp"), axis=0, tiled=True),
        lax.all_gather(up_low, ("dp", "fsdp"), axis=0, tiled=True),
        lax.all_gather(down_low, ("dp", "fsdp"), axis=0, tiled=True),
    )
    grad_down = jnp.dot(active.T, cotangent, preferred_element_type=jnp.float32)
    sum_down = jnp.sum(cotangent, axis=0, dtype=jnp.float32)
    grad_active = jnp.dot(cotangent, down_back.T, preferred_element_type=jnp.float32)
    grad_hidden = gelu_pull(grad_active)[0].astype(jnp.bfloat16)
    grad_up = jnp.dot(second.T, grad_hidden, preferred_element_type=jnp.float32)
    sum_up = jnp.sum(grad_hidden, axis=0, dtype=jnp.float32)
    grad_second = jnp.dot(grad_hidden, up_back.T, preferred_element_type=jnp.float32)
    middle_part, grad_gain_two, grad_bias_two = norm_two_pull(grad_second)
    grad_middle = cotangent.astype(jnp.float32) + middle_part
    grad_branch = grad_middle.astype(jnp.bfloat16)
    grad_proj = jnp.dot(mixture.T, grad_branch, preferred_element_type=jnp.float32)
    sum_proj = jnp.sum(grad_branch, axis=0, dtype=jnp.float32)
    grad_mixture = jnp.dot(grad_branch, proj_back.T, preferred_element_type=jnp.float32).astype(
        jnp.bfloat16
    )
    grad_mixture = grad_mixture.reshape(clouds_here, P_SIZE, HEADS, HD)
    again_scores = masked_scores(queries, keys_part, allowed)
    probs = jnp.exp(again_scores - log_total)
    grad_probs = jnp.einsum(
        "cqhd,ckhd->chqk", grad_mixture, values, preferred_element_type=jnp.float32
    )
    delta_sum = jnp.sum(probs * grad_probs, axis=-1, keepdims=True)
    grad_scores = (probs * (grad_probs - delta_sum)).astype(jnp.bfloat16)
    grad_values = jnp.einsum(
        "chqk,cqhd->ckhd",
        probs.astype(jnp.bfloat16),
        grad_mixture,
        preferred_element_type=jnp.float32,
    )
    grad_queries = jnp.einsum(
        "chqk,ckhd->cqhd", grad_scores, keys_part, preferred_element_type=jnp.float32
    ) * HD ** (-0.5)
    grad_keys = jnp.einsum(
        "chqk,cqhd->ckhd", grad_scores, queries, preferred_element_type=jnp.float32
    ) * HD ** (-0.5)
    grad_packed = (
        jnp.stack((grad_queries, grad_keys, grad_values), axis=2)
        .reshape(rows_here, 3 * D)
        .astype(jnp.bfloat16)
    )
    grad_qkv = jnp.dot(normed.T, grad_packed, preferred_element_type=jnp.float32)
    grad_normed = jnp.dot(grad_packed, qkv_back.T, preferred_element_type=jnp.float32)
    input_part, grad_gain_one, grad_bias_one = norm_one_pull(grad_normed)
    input_grad = grad_middle + input_part
    grad_vector = jnp.concatenate(
        [grad_gain_one, grad_bias_one, grad_gain_two, grad_bias_two, sum_proj, sum_down, sum_up]
    )
    summed = (
        lax.psum_scatter(grad_qkv, ("dp", "fsdp"), scatter_dimension=0, tiled=True),
        lax.psum_scatter(grad_proj, ("dp", "fsdp"), scatter_dimension=0, tiled=True),
        lax.psum_scatter(grad_up, ("dp", "fsdp"), scatter_dimension=0, tiled=True),
        lax.psum_scatter(grad_down, ("dp", "fsdp"), scatter_dimension=0, tiled=True),
        lax.psum_scatter(grad_vector, ("dp", "fsdp"), scatter_dimension=0, tiled=True),
    )
    squares = jnp.float32(0.0)
    for member in summed:
        squares = squares + jnp.sum(member * member)
    clip_norm = jnp.sqrt(lax.psum(squares, ("dp", "fsdp")))
    factor = 1.0 / clip_norm
    qkv_new, qkv_first_new, qkv_second_new = adam_step(
        qkv_weight, qkv_first, qkv_second, summed[0] * factor, matrix_rates[0], decay_rate
    )
    proj_new, proj_first_new, proj_second_new = adam_step(
        proj_weight, proj_first, proj_second, summed[1] * factor, matrix_rates[1], decay_rate
    )
    up_new, up_first_new, up_second_new = adam_step(
        up_weight, up_first, up_second, summed[2] * factor, matrix_rates[2], decay_rate
    )
    down_new, down_first_new, down_second_new = adam_step(
        down_weight, down_first, down_second, summed[3] * factor, matrix_rates[3], decay_rate
    )
    vector_new, vector_first_new, vector_second_new = adam_step(
        vectors, vector_first, vector_second, summed[4] * factor, vector_rate, 0.0
    )
    return (
        block_out,
        input_grad,
        clip_norm,
        qkv_new,
        qkv_first_new,
        qkv_second_new,
        proj_new,
        proj_first_new,
        proj_second_new,
        up_new,
        up_first_new,
        up_second_new,
        down_new,
        down_first_new,
        down_second_new,
        vector_new,
        vector_first_new,
        vector_second_new,
    )


def solution(mesh):
    placed = (
        P(("dp", "fsdp"), None),
        P(("dp", "fsdp"), None),
        P(("dp", "fsdp"), None, None),
        P(("dp", "fsdp"), None),
        P(("dp", "fsdp"), None),
        P(("dp", "fsdp"), None),
        P(("dp", "fsdp"), None),
        P(("dp", "fsdp"), None),
        P(("dp", "fsdp"), None),
        P(("dp", "fsdp"), None),
        P(("dp", "fsdp"), None),
        P(("dp", "fsdp"), None),
        P(("dp", "fsdp"), None),
        P(("dp", "fsdp"), None),
        P(("dp", "fsdp"), None),
        P(("dp", "fsdp")),
        P(("dp", "fsdp")),
        P(("dp", "fsdp")),
    )
    return jax.shard_map(
        per_device,
        mesh=mesh,
        in_specs=placed,
        out_specs=(
            P(("dp", "fsdp"), None),
            P(("dp", "fsdp"), None),
            P(),
            P(("dp", "fsdp"), None),
            P(("dp", "fsdp"), None),
            P(("dp", "fsdp"), None),
            P(("dp", "fsdp"), None),
            P(("dp", "fsdp"), None),
            P(("dp", "fsdp"), None),
            P(("dp", "fsdp"), None),
            P(("dp", "fsdp"), None),
            P(("dp", "fsdp"), None),
            P(("dp", "fsdp"), None),
            P(("dp", "fsdp"), None),
            P(("dp", "fsdp"), None),
            P(("dp", "fsdp")),
            P(("dp", "fsdp")),
            P(("dp", "fsdp")),
        ),
        check_vma=False,
    )
```

profile of v0, /device:TPU:0, one launch (start us, length us, event | category | flops | bytes accessed | tf_op | source)
XLA Modules:
  0.0 689.9 jit_solution(5991985570450772229)
XLA Ops:
  11.3 42.1 %all-reduce = bf16[3840]{0:T(1024)(128)(2,1)S(1)} all-reduce(bf16[3840]{0:T(1024)(128)(2,1)S(1)} %dynamic-update-slice), channel_id=1, replica_groups=mesh['dp'=8,'fsdp'=4] {'dp','fsdp'}, use_global_device_ids=true, to_apply=%add | all-reduce | flops 3840 | bytes 15360
  54.0 1.9 copy.90
  57.3 43.9 %all-gather = bf16[32,12,1152]{2,1,0:T(8,128)(2,1)S(1)} all-gather(bf16[1,12,1152]{2,1,0:T(8,128)(2,1)S(1)} %convert_bitcast_fusion.3), channel_id=1, replica_groups=mesh['dp'=8,'fsdp'=4] {'dp','fsdp'}, dimensions={0}, use_global_device_ids=true | all-gather | bytes 912384 | tf_op jit(solution)/shard_map/all_gather | solution.py:96
  102.3 5.9 convolution_convert_fusion
  108.2 6.7 copy.91
  114.9 14.4 %reshape.139 = bf16[32,64,3,6,64]{1,0,4,3,2:T(8,128)(2,1)} reshape(bf16[2048,1152]{0,1:T(8,128)(2,1)} %copy.91) | data formatting | bytes 9437184 | tf_op jit(solution)/shard_map/reshape | solution.py:111
  129.4 6.4 fusion.69
  135.8 5.0 copy.131
  140.8 5.1 copy.132
  146.6 4.6 fusion.71
  155.5 4.3 convert_bitcast_fusion.1
  159.8 3.6 copy.97
  163.4 4.7 convert_element_type.86
  168.2 40.4 %all-gather.1 = bf16[32,12,384]{2,1,0:T(8,128)(2,1)} all-gather(bf16[1,12,384]{2,1,0:T(8,128)(2,1)S(1)} %convert_bitcast_fusion.4), channel_id=1, replica_groups=mesh['dp'=8,'fsdp'=4] {'dp','fsdp'}, dimensions={0}, use_global_device_ids=true | all-gather | bytes 304128 | tf_op jit(solution)/shard_map/all_gather | solution.py:97
  212.8 2.7 copy.99
  215.5 3.0 reshape.148
  218.6 34.8 %multiply_convert_fusion = (bf16[2048,1536]{1,0:T(8,128)(2,1)}, f32[2048,1536]{1,0:T(8,128)}, f32[2048,1536]{1,0:T(8,128)}) fusion(f32[1536]{0:T(1024)S(1)} %slice.48, bf16[384,1536]{1,0:T(8,128)(2,1)} %reshape.148, f32[2048,384]{0,1:T(8,128)S(1)} %copy-done.4, f32[384]{0:T(512)S(1)} %get-tuple-element.110, f32[384]{0:T(512)S(1)} %get-tuple-element.109, ...), kind=kOutput, calls=%fused_computation.4 | convolution fusion | flops 2627469312 | bytes 35808256 | tf_op jit(solution)/shard_map/dot_general | solution.py:128
  253.4 15.0 %convert_reduce_fusion = (f32[1536]{0:T(1024)}, bf16[2048,1536]{1,0:T(8,128)(2,1)S(1)}) fusion(f32[2048,1536]{1,0:T(8,128)} %get-tuple-element.102, bf16[2048,384]{1,0:T(8,128)(2,1)} %param.19, bf16[1536,384]{1,0:T(8,128)(2,1)} %all-gather.6.cloned.1.call-done, f32[2048,1536]{1,0:T(8,128)} %get-tuple-element.118, f32[1536]{0:T(1024)S(1)} %slice.48), kind=kOutput, calls=%fused_computation.2 | convolution fusion | flops 2469394944 | bytes 34222080 | tf_op jit(solution)/shard_map/dot_general | solution.py:141
  268.4 5.7 fusion.74
  274.1 3.6 copy.100
  277.8 3.5 multiply_reduce_fusion.1
  286.4 3.7 reshape.149
  290.1 6.5 copy.110
  296.7 11.6 %multiply_reduce_fusion = (f32[32,6,64]{2,1,0:T(8,128)S(1)}, f32[32,6,64,64]{2,3,1,0:T(8,128)}) fusion(f32[32,6,64,64]{2,3,1,0:T(8,128)} %copy-done, f32[32,6,64]{2,1,0:T(8,128)S(1)} %copy-done.24, bf16[32,64,6,64]{1,3,2,0:T(8,128)(2,1)} %copy.110, bf16[32,64,1,6,64]{1,0,4,3,2:T(8,128)(2,1)} %get-tuple-element.103), kind=kOutput, calls=%fused_computation.23 | convolution fusion | flops 103010304 | bytes 9535488 | tf_op jit(solution)/shard_map/cqhd,ckhd->chqk/dot_general | solution.py:157
  308.2 6.8 multiply_convert_fusion.3
  315.0 5.0 fusion.24
  320.1 2.7 fusion.25
  322.8 3.6 convert_bitcast_fusion
  326.6 4.1 fusion.58
  330.7 7.9 %pad_maximum_fusion = bf16[32,64,3,6,64]{4,1,3,0,2:T(8,128)(2,1)} fusion(bf16[32,64,1,6,64]{4,1,3,0,2:T(8,128)(2,1)} %convert_bitcast_fusion, bf16[32,64,1,6,64]{4,1,3,0,2:T(8,128)(2,1)} %fusion.25, bf16[32,64,1,6,64]{4,1,3,0,2:T(8,128)(2,1)S(1)} %copy-done.19), kind=kLoop, calls=%fused_computation.18 | loop fusion | flops 4718592 | bytes 9437184 | tf_op jit(solution)/shard_map/stack | solution.py:175
  338.6 13.5 %copy.113 = bf16[32,64,3,6,64]{1,0,4,3,2:T(8,128)(2,1)} copy(bf16[32,64,3,6,64]{4,1,3,0,2:T(8,128)(2,1)} %pad_maximum_fusion) | data formatting | bytes 9437184 | tf_op jit(solution)/shard_map/stack | solution.py:175
  352.1 13.9 %convert_element_type.99 = bf16[2048,1152]{0,1:T(8,128)(2,1)} reshape(bf16[32,64,3,6,64]{1,0,4,3,2:T(8,128)(2,1)} %copy.113) | data formatting | bytes 9437184 | tf_op jit(solution)/shard_map/convert_element_type | solution.py:177
  366.0 7.6 %fusion.73 = (f32[384]{0:T(512)}, f32[2048,384]{1,0:T(8,128)}) fusion(bf16[2048,1152]{0,1:T(8,128)(2,1)} %convert_element_type.99, bf16[384,1152]{1,0:T(8,128)(2,1)S(1)} %copy-done.29), kind=kOutput, calls=%fused_computation.131 | convolution fusion | flops 1812725376 | bytes 8750592 | tf_op jit(solution)/shard_map/dot_general | solution.py:180
  373.6 2.5 fusion.55
  378.0 80.8 %fusion.60 = (f32[16,1152]{1,0:T(8,128)S(1)}, f32[16,384]{1,0:T(8,128)S(1)}, f32[16,1536]{1,0:T(8,128)S(1)}) fusion(f32[384,1152]{1,0:T(8,128)S(1)} %fusion.55, f32[384,384]{1,0:T(8,128)} %fusion.75, f32[384,1536]{1,0:T(8,128)} %fusion.58), kind=kCustom, calls=%all-reduce-scatter.3 | all-reduce-scatter fusion | flops 1572865 | bytes 4915200
  463.3 1.9 collective-permute-start.13
  465.2 3.6 copy.114
  468.8 2.5 fusion.21
  471.4 2.1 collective-permute-start.15
  473.4 7.7 %fusion.76 = f32[1536,384]{1,0:T(8,128)} fusion(bf16[2048,1536]{1,0:T(8,128)(2,1)} %get-tuple-element.101, bf16[2048,384]{1,0:T(8,128)(2,1)S(1)} %copy-done.25), kind=kOutput, calls=%fused_computation.134 | convolution fusion | flops 2415919104 | bytes 10223616 | tf_op jit(solution)/shard_map/dot_general | solution.py:139
  481.2 3.4 fusion.19
  487.3 6.1 convert_reduce_fusion.2
  493.4 6.8 add_convert_fusion.1
  501.6 3.9 collective-permute-start.14
  505.5 4.8 collective-permute-start.8
  510.3 3.4 collective-permute-start.9
  513.7 1.9 collective-permute-start.7
  517.0 2.4 copy.118
  519.4 3.6 collective-permute-start
  522.9 2.8 collective-permute-start.1
  527.6 2.9 collective-permute-start.3
  533.1 2.0 collective-permute-done.23
  536.4 4.0 collective-permute-start.17
  540.4 5.3 collective-permute-start.4
  545.7 4.0 collective-permute-start.5
  549.7 1.9 collective-permute-start.6
  554.9 2.2 collective-permute-start.19
  558.5 2.8 collective-permute-start.21
  561.4 2.9 collective-permute-start.22
  565.6 37.4 %all-reduce.4 = f32[3840]{0:T(1024)S(1)} all-reduce(f32[3840]{0:T(1024)} %constant_dynamic-update-slice_fusion), channel_id=6, replica_groups=mesh['dp'=8,'fsdp'=4] {'dp','fsdp'}, use_global_device_ids=true, to_apply=%region_26.27.clone | all-reduce | flops 3840 | bytes 30720
  603.7 5.9 concatenate.5
  610.2 5.4 concatenate.4
  618.9 8.0 %concatenate.6 = f32[140,1536]{1,0:T(8,128)S(1)} concatenate(f32[12,1536]{1,0:T(8,128)} %copy-done.38, f32[16,1536]{1,0:T(8,128)} %collective-permute-done.22, f32[16,1536]{1,0:T(8,128)} %copy-done.44, f32[16,1536]{1,0:T(8,128)} %copy-done.43, f32[16,1536]{1,0:T(8,128)} %copy-done.42, f32[16,1536]{1,0:T(8,128)} %copy-done.41, f32[16,1536]{1,0:T(8,128)} %copy-done.40, ...), dimensions={0} | concatenate | bytes 1720320
  632.7 40.9 %psum.7 = f32[]{:T(128)} all-reduce(f32[]{:T(128)S(6)} %add.199), channel_id=1, replica_groups=mesh['dp'=8,'fsdp'=4] {'dp','fsdp'}, use_global_device_ids=true, to_apply=%region_28.29 | all-reduce | flops 1 | bytes 8 | tf_op jit(solution)/shard_map/psum | solution.py:196
  (248 shorter events, 59.5 us)
Async XLA Ops:
  7.2 208.4 %all-gather.8.cloned.1.call-start = ((), (), s32[]{:S(2)}) async-start(), calls=%async_computation.3 | async-start | bytes 1622016 | tf_op jit(solution)/shard_map/all_gather | solution.py:98
  8.8 244.6 %all-gather.6.cloned.1.call-start = ((), (), s32[]{:S(2)}) async-start(), calls=%async_computation.1 | async-start | bytes 1216512 | tf_op jit(solution)/shard_map/all_gather | solution.py:99
  10.4 617.9 %reduce-scatter.8.cloned.1.call-start = ((), (), s32[]{:S(2)}) async-start(), calls=%async_computation.2 | async-start | bytes 2433024 | tf_op jit(solution)/shard_map/reduce_scatter | solution.py:190
  54.0 48.3 %copy-start.56 = (f32[384]{0:T(512)}, f32[384]{0:T(512)S(1)}, u32[]{:S(2)}) copy-start(f32[384]{0:T(512)S(1)} %get-tuple-element.112) | copy-start | bytes 4612
  54.0 48.3 %copy-start.66 = (f32[384]{0:T(512)}, f32[384]{0:T(512)S(1)}, u32[]{:S(2)}) copy-start(f32[384]{0:T(512)S(1)} %get-tuple-element.113) | copy-start | bytes 4612
  56.0 153.6 %copy-start.1 = (bf16[2048,384]{0,1:T(8,128)(2,1)}, bf16[2048,384]{0,1:T(8,128)(2,1)S(1)}, u32[]{:S(2)}) copy-start(bf16[2048,384]{0,1:T(8,128)(2,1)S(1)} %copy.90) | copy-start | bytes 4718596
  56.3 52.0 %copy-start.36 = (f32[2048]{0:T(1024)}, f32[2048]{0:T(1024)S(1)}, u32[]{:S(2)}) copy-start(f32[2048]{0:T(1024)S(1)} %broadcast_multiply_fusion.1) | copy-start | bytes 24580
  57.3 50.9 %copy-start.47 = (f32[2048]{0:T(1024)}, f32[2048]{0:T(1024)S(1)}, u32[]{:S(2)}) copy-start(f32[2048]{0:T(1024)S(1)} %fusion.52) | copy-start | bytes 24580
  168.1 42.7 %copy-start.21 = (bf16[2048,384]{0,1:T(8,128)(2,1)}, bf16[2048,384]{0,1:T(8,128)(2,1)S(1)}, u32[]{:S(2)}) copy-start(bf16[2048,384]{0,1:T(8,128)(2,1)S(1)} %convert_element_type.86) | copy-start | bytes 4718596
  253.4 15.1 %copy-start.27 = (bf16[384,1536]{1,0:T(8,128)(2,1)S(1)}, bf16[384,1536]{1,0:T(8,128)(2,1)}, u32[]{:S(2)}) copy-start(bf16[384,1536]{1,0:T(8,128)(2,1)} %reshape.148) | copy-start | bytes 3538948
  290.1 18.1 %slice-start = ((s8[6291456]{0:T(1024)(128)(4,1)}), s8[2097152]{0:T(1024)(128)(4,1)S(1)}, s32[]{:S(2)}) async-start(s8[6291456]{0:T(1024)(128)(4,1)} %bitcast.84), calls=%async_computation.4 | async-start | bytes 4194304
  296.7 11.6 %slice-start.1 = ((s8[6291456]{0:T(1024)(128)(4,1)}), s8[4194304]{0:T(1024)(128)(4,1)S(1)}, s32[]{:S(2)}) async-start(s8[6291456]{0:T(1024)(128)(4,1)} %bitcast.84), calls=%async_computation.5 | async-start | bytes 8388608
  308.2 6.8 copy-start.11
  352.1 13.9 %copy-start.29 = (bf16[384,1152]{1,0:T(8,128)(2,1)S(1)}, bf16[384,1152]{1,0:T(8,128)(2,1)}, u32[]{:S(2)}) copy-start(bf16[384,1152]{1,0:T(8,128)(2,1)} %reshape.144) | copy-start | bytes 2654212
  365.9 7.6 %copy-start.2 = (bf16[2048,384]{0,1:T(8,128)(2,1)S(1)}, bf16[2048,384]{0,1:T(8,128)(2,1)}, u32[]{:S(2)}) copy-start(bf16[2048,384]{0,1:T(8,128)(2,1)} %copy-done.1) | copy-start | bytes 4718596
  365.9 7.6 %copy-start.23 = (bf16[2048,1152]{0,1:T(8,128)(2,1)S(1)}, bf16[2048,1152]{0,1:T(8,128)(2,1)}, u32[]{:S(2)}) copy-start(bf16[2048,1152]{0,1:T(8,128)(2,1)} %convert_element_type.99) | copy-start | bytes 14155780
  365.9 7.6 %copy-start.37 = (f32[2048]{0:T(1024)S(1)}, f32[2048]{0:T(1024)}, u32[]{:S(2)}) copy-start(f32[2048]{0:T(1024)} %copy-done.36) | copy-start | bytes 24580
  365.9 7.6 %copy-start.48 = (f32[2048]{0:T(1024)S(1)}, f32[2048]{0:T(1024)}, u32[]{:S(2)}) copy-start(f32[2048]{0:T(1024)} %copy-done.47) | copy-start | bytes 24580
  366.0 7.6 %copy-start.57 = (f32[384]{0:T(512)S(1)}, f32[384]{0:T(512)}, u32[]{:S(2)}) copy-start(f32[384]{0:T(512)} %copy-done.56) | copy-start | bytes 4612
  366.0 7.6 %copy-start.67 = (f32[384]{0:T(512)S(1)}, f32[384]{0:T(512)}, u32[]{:S(2)}) copy-start(f32[384]{0:T(512)} %copy-done.66) | copy-start | bytes 4612
  459.4 46.0 %collective-permute-start.10 = (f32[16,384]{1,0:T(8,128)S(1)}, f32[16,384]{1,0:T(8,128)S(1)}, u32[]{:S(2)}, u32[]{:S(2)}) collective-permute-start(f32[16,384]{1,0:T(8,128)S(1)} %get-tuple-element.80), channel_id=1, source_target_pairs={{0,3},{1,4},{2,5},{3,6},{4,7},{5,8},{6,9},{7,10},{8,11},{9,12},{10... | collective-permute-start | bytes 73736
  460.7 49.5 %collective-permute-start.11 = (f32[16,384]{1,0:T(8,128)S(1)}, f32[16,384]{1,0:T(8,128)S(1)}, u32[]{:S(2)}, u32[]{:S(2)}) collective-permute-start(f32[16,384]{1,0:T(8,128)S(1)} %get-tuple-element.80), channel_id=1, source_target_pairs={{0,4},{1,5},{2,6},{3,7},{4,8},{5,9},{6,10},{7,11},{8,12},{9,13},{1... | collective-permute-start | bytes 73736
  462.0 51.7 %collective-permute-start.12 = (f32[16,384]{1,0:T(8,128)S(1)}, f32[16,384]{1,0:T(8,128)S(1)}, u32[]{:S(2)}, u32[]{:S(2)}) collective-permute-start(f32[16,384]{1,0:T(8,128)S(1)} %get-tuple-element.80), channel_id=1, source_target_pairs={{0,5},{1,6},{2,7},{3,8},{4,9},{5,10},{6,11},{7,12},{8,13},{9,14},{... | collective-permute-start | bytes 73736
  463.3 56.0 %collective-permute-start.13 = (f32[16,384]{1,0:T(8,128)S(1)}, f32[16,384]{1,0:T(8,128)}, u32[]{:S(2)}, u32[]{:S(2)}) collective-permute-start(f32[16,384]{1,0:T(8,128)S(1)} %get-tuple-element.80), channel_id=1, source_target_pairs={{0,6},{1,7},{2,8},{3,9},{4,10},{5,11},{6,12},{7,13},{8,14},{9,15},... | collective-permute-start | bytes 73736
  471.4 30.2 %collective-permute-start.15 = (f32[12,384]{1,0:T(8,128)}, f32[12,384]{1,0:T(8,128)}, u32[]{:S(2)}, u32[]{:S(2)}) collective-permute-start(f32[12,384]{1,0:T(8,128)} %slice.51), channel_id=1, source_target_pairs={{0,8},{1,9},{2,10},{3,11},{4,12},{5,13},{6,14},{7,15},{8,16},{9,17... | collective-permute-start | bytes 55304
  473.4 7.8 %copy-start.52 = (f32[2048]{0:T(1024)S(1)}, f32[2048]{0:T(1024)}, u32[]{:S(2)}) copy-start(f32[2048]{0:T(1024)} %copy-done.51) | copy-start | bytes 24580
  493.4 6.9 copy-start.62
  493.4 22.2 %copy-start.68 = (f32[384]{0:T(512)S(1)}, f32[384]{0:T(512)}, u32[]{:S(2)}) copy-start(f32[384]{0:T(512)} %get-tuple-element.123) | copy-start | bytes 4612
  493.4 23.5 %copy-start.20 = (f32[2048,384]{0,1:T(8,128)S(1)}, f32[2048,384]{0,1:T(8,128)}, u32[]{:S(2)}) copy-start(f32[2048,384]{0,1:T(8,128)} %get-tuple-element.107) | copy-start | bytes 9437188
  501.6 21.3 %collective-permute-start.14 = (f32[16,384]{1,0:T(8,128)S(1)}, f32[16,384]{1,0:T(8,128)}, u32[]{:S(2)}, u32[]{:S(2)}) collective-permute-start(f32[16,384]{1,0:T(8,128)S(1)} %get-tuple-element.80), channel_id=1, source_target_pairs={{0,7},{1,8},{2,9},{3,10},{4,11},{5,12},{6,13},{7,14},{8,15},{9,16}... | collective-permute-start | bytes 73736
  505.5 20.3 %collective-permute-start.8 = (f32[16,384]{1,0:T(8,128)S(1)}, f32[16,384]{1,0:T(8,128)}, u32[]{:S(2)}, u32[]{:S(2)}) collective-permute-start(f32[16,384]{1,0:T(8,128)S(1)} %get-tuple-element.80), channel_id=1, source_target_pairs={{0,1},{1,2},{2,3},{3,4},{4,5},{5,6},{6,7},{7,8},{8,9},{9,10},{10,1... | collective-permute-start | bytes 73736
  510.3 6.6 copy-start.59
  510.3 17.3 %collective-permute-start.9 = (f32[16,384]{1,0:T(8,128)S(1)}, f32[16,384]{1,0:T(8,128)}, u32[]{:S(2)}, u32[]{:S(2)}) collective-permute-start(f32[16,384]{1,0:T(8,128)S(1)} %get-tuple-element.80), channel_id=1, source_target_pairs={{0,2},{1,3},{2,4},{3,5},{4,6},{5,7},{6,8},{7,9},{8,10},{9,11},{10,... | collective-permute-start | bytes 73736
  513.7 16.8 %collective-permute-start.7 = (f32[12,1152]{1,0:T(8,128)S(1)}, f32[12,1152]{1,0:T(8,128)}, u32[]{:S(2)}, u32[]{:S(2)}) collective-permute-start(f32[12,1152]{1,0:T(8,128)S(1)} %slice.50), channel_id=1, source_target_pairs={{0,8},{1,9},{2,10},{3,11},{4,12},{5,13},{6,14},{7,15},{8,16},{9,17... | collective-permute-start | bytes 165896
  517.0 14.9 %copy-start.61 = (f32[384]{0:T(512)S(1)}, f32[384]{0:T(512)}, u32[]{:S(2)}) copy-start(f32[384]{0:T(512)} %get-tuple-element.97) | copy-start | bytes 4612
  517.0 34.7 %copy-start.63 = (f32[384]{0:T(512)S(1)}, f32[384]{0:T(512)}, u32[]{:S(2)}) copy-start(f32[384]{0:T(512)} %get-tuple-element.106) | copy-start | bytes 4612
  517.0 47.3 %copy-start.64 = (f32[1536]{0:T(1024)S(1)}, f32[1536]{0:T(1024)}, u32[]{:S(2)}) copy-start(f32[1536]{0:T(1024)} %get-tuple-element.125) | copy-start | bytes 18436
  519.4 111.8 %copy-start.26 = (bf16[2048,384]{0,1:T(8,128)(2,1)S(1)}, bf16[2048,384]{0,1:T(8,128)(2,1)}, u32[]{:S(2)}) copy-start(bf16[2048,384]{0,1:T(8,128)(2,1)} %add_convert_fusion.1) | copy-start | bytes 4718596
  519.4 17.0 %collective-permute-start = (f32[16,1152]{1,0:T(8,128)S(1)}, f32[16,1152]{1,0:T(8,128)S(1)}, u32[]{:S(2)}, u32[]{:S(2)}) collective-permute-start(f32[16,1152]{1,0:T(8,128)S(1)} %get-tuple-element.79), channel_id=1, source_target_pairs={{0,1},{1,2},{2,3},{3,4},{4,5},{5,6},{6,7},{7,8},{8,9},{9,10},{10,1... | collective-permute-start | bytes 221192
  522.9 17.5 %collective-permute-start.1 = (f32[16,1152]{1,0:T(8,128)S(1)}, f32[16,1152]{1,0:T(8,128)S(1)}, u32[]{:S(2)}, u32[]{:S(2)}) collective-permute-start(f32[16,1152]{1,0:T(8,128)S(1)} %get-tuple-element.79), channel_id=1, source_target_pairs={{0,2},{1,3},{2,4},{3,5},{4,6},{5,7},{6,8},{7,9},{8,10},{9,11},{10,... | collective-permute-start | bytes 221192
  525.7 20.0 %collective-permute-start.2 = (f32[16,1152]{1,0:T(8,128)S(1)}, f32[16,1152]{1,0:T(8,128)S(1)}, u32[]{:S(2)}, u32[]{:S(2)}) collective-permute-start(f32[16,1152]{1,0:T(8,128)S(1)} %get-tuple-element.79), channel_id=1, source_target_pairs={{0,3},{1,4},{2,5},{3,6},{4,7},{5,8},{6,9},{7,10},{8,11},{9,12},{10... | collective-permute-start | bytes 221192
  527.6 22.2 %collective-permute-start.3 = (f32[16,1152]{1,0:T(8,128)S(1)}, f32[16,1152]{1,0:T(8,128)S(1)}, u32[]{:S(2)}, u32[]{:S(2)}) collective-permute-start(f32[16,1152]{1,0:T(8,128)S(1)} %get-tuple-element.79), channel_id=1, source_target_pairs={{0,4},{1,5},{2,6},{3,7},{4,8},{5,9},{6,10},{7,11},{8,12},{9,13},{1... | collective-permute-start | bytes 221192
  530.5 4.6 collective-permute-start.23
  535.1 67.9 %copy-start.38 = (f32[12,1536]{1,0:T(8,128)}, f32[12,1536]{1,0:T(8,128)S(1)}, u32[]{:S(2)}) copy-start(f32[12,1536]{1,0:T(8,128)S(1)} %collective-permute-done.23) | copy-start | bytes 221188
  535.1 23.4 %collective-permute-start.16 = (f32[16,1536]{1,0:T(8,128)S(1)}, f32[16,1536]{1,0:T(8,128)S(1)}, u32[]{:S(2)}, u32[]{:S(2)}) collective-permute-start(f32[16,1536]{1,0:T(8,128)S(1)} %get-tuple-element.81), channel_id=1, source_target_pairs={{0,1},{1,2},{2,3},{3,4},{4,5},{5,6},{6,7},{7,8},{8,9},{9,10},{10,1... | collective-permute-start | bytes 294920
  536.4 25.0 %collective-permute-start.17 = (f32[16,1536]{1,0:T(8,128)S(1)}, f32[16,1536]{1,0:T(8,128)S(1)}, u32[]{:S(2)}, u32[]{:S(2)}) collective-permute-start(f32[16,1536]{1,0:T(8,128)S(1)} %get-tuple-element.81), channel_id=1, source_target_pairs={{0,2},{1,3},{2,4},{3,5},{4,6},{5,7},{6,8},{7,9},{8,10},{9,11},{10,... | collective-permute-start | bytes 294920
  540.4 12.6 %collective-permute-start.4 = (f32[16,1152]{1,0:T(8,128)S(1)}, f32[16,1152]{1,0:T(8,128)S(1)}, u32[]{:S(2)}, u32[]{:S(2)}) collective-permute-start(f32[16,1152]{1,0:T(8,128)S(1)} %get-tuple-element.79), channel_id=1, source_target_pairs={{0,5},{1,6},{2,7},{3,8},{4,9},{5,10},{6,11},{7,12},{8,13},{9,14},{... | collective-permute-start | bytes 221192
  545.7 7.3 %copy-start.54 = (f32[16,1152]{1,0:T(8,128)}, f32[16,1152]{1,0:T(8,128)S(1)}, u32[]{:S(2)}) copy-start(f32[16,1152]{1,0:T(8,128)S(1)} %collective-permute-done.2) | copy-start | bytes 221188
  545.7 9.1 %collective-permute-start.5 = (f32[16,1152]{1,0:T(8,128)S(1)}, f32[16,1152]{1,0:T(8,128)}, u32[]{:S(2)}, u32[]{:S(2)}) collective-permute-start(f32[16,1152]{1,0:T(8,128)S(1)} %get-tuple-element.79), channel_id=1, source_target_pairs={{0,6},{1,7},{2,8},{3,9},{4,10},{5,11},{6,12},{7,13},{8,14},{9,15},... | collective-permute-start | bytes 221192
  549.7 7.3 %collective-permute-start.6 = (f32[16,1152]{1,0:T(8,128)S(1)}, f32[16,1152]{1,0:T(8,128)}, u32[]{:S(2)}, u32[]{:S(2)}) collective-permute-start(f32[16,1152]{1,0:T(8,128)S(1)} %get-tuple-element.79), channel_id=1, source_target_pairs={{0,7},{1,8},{2,9},{3,10},{4,11},{5,12},{6,13},{7,14},{8,15},{9,16}... | collective-permute-start | bytes 221192
  553.0 64.6 %collective-permute-start.18 = (f32[16,1536]{1,0:T(8,128)S(1)}, f32[16,1536]{1,0:T(8,128)S(1)}, u32[]{:S(2)}, u32[]{:S(2)}) collective-permute-start(f32[16,1536]{1,0:T(8,128)S(1)} %get-tuple-element.81), channel_id=1, source_target_pairs={{0,3},{1,4},{2,5},{3,6},{4,7},{5,8},{6,9},{7,10},{8,11},{9,12},{10... | collective-permute-start | bytes 294920
  554.9 62.7 %collective-permute-start.19 = (f32[16,1536]{1,0:T(8,128)S(1)}, f32[16,1536]{1,0:T(8,128)S(1)}, u32[]{:S(2)}, u32[]{:S(2)}) collective-permute-start(f32[16,1536]{1,0:T(8,128)S(1)} %get-tuple-element.81), channel_id=1, source_target_pairs={{0,4},{1,5},{2,6},{3,7},{4,8},{5,9},{6,10},{7,11},{8,12},{9,13},{1... | collective-permute-start | bytes 294920
  557.1 60.5 %collective-permute-start.20 = (f32[16,1536]{1,0:T(8,128)S(1)}, f32[16,1536]{1,0:T(8,128)S(1)}, u32[]{:S(2)}, u32[]{:S(2)}) collective-permute-start(f32[16,1536]{1,0:T(8,128)S(1)} %get-tuple-element.81), channel_id=1, source_target_pairs={{0,5},{1,6},{2,7},{3,8},{4,9},{5,10},{6,11},{7,12},{8,13},{9,14},{... | collective-permute-start | bytes 294920
  558.5 44.5 %copy-start.39 = (f32[16,1536]{1,0:T(8,128)}, f32[16,1536]{1,0:T(8,128)S(1)}, u32[]{:S(2)}) copy-start(f32[16,1536]{1,0:T(8,128)S(1)} %collective-permute-done.16) | copy-start | bytes 294916
  558.5 59.1 %collective-permute-start.21 = (f32[16,1536]{1,0:T(8,128)S(1)}, f32[16,1536]{1,0:T(8,128)S(1)}, u32[]{:S(2)}, u32[]{:S(2)}) collective-permute-start(f32[16,1536]{1,0:T(8,128)S(1)} %get-tuple-element.81), channel_id=1, source_target_pairs={{0,6},{1,7},{2,8},{3,9},{4,10},{5,11},{6,12},{7,13},{8,14},{9,15},... | collective-permute-start | bytes 294920
  561.4 41.6 %copy-start.40 = (f32[16,1536]{1,0:T(8,128)}, f32[16,1536]{1,0:T(8,128)S(1)}, u32[]{:S(2)}) copy-start(f32[16,1536]{1,0:T(8,128)S(1)} %collective-permute-done.17) | copy-start | bytes 294916
  561.4 57.5 %collective-permute-start.22 = (f32[16,1536]{1,0:T(8,128)S(1)}, f32[16,1536]{1,0:T(8,128)}, u32[]{:S(2)}, u32[]{:S(2)}) collective-permute-start(f32[16,1536]{1,0:T(8,128)S(1)} %get-tuple-element.81), channel_id=1, source_target_pairs={{0,7},{1,8},{2,9},{3,10},{4,11},{5,12},{6,13},{7,14},{8,15},{9,16}... | collective-permute-start | bytes 294920
  609.6 8.0 %copy-start.31 = (f32[140,384]{1,0:T(8,128)}, f32[140,384]{1,0:T(8,128)S(1)}, u32[]{:S(2)}) copy-start(f32[140,384]{1,0:T(8,128)S(1)} %concatenate.5) | copy-start | bytes 645124
  610.2 65.5 %copy-start.30 = (f32[12,1536]{1,0:T(8,128)S(1)}, f32[12,1536]{1,0:T(8,128)}, u32[]{:S(2)}) copy-start(f32[12,1536]{1,0:T(8,128)} %param.27) | copy-start | bytes 221188
  615.6 61.8 %copy-start.46 = (f32[12,384]{1,0:T(8,128)S(1)}, f32[12,384]{1,0:T(8,128)}, u32[]{:S(2)}) copy-start(f32[12,384]{1,0:T(8,128)} %param.24) | copy-start | bytes 55300
  615.6 63.2 %copy-start.33 = (f32[12,1152]{1,0:T(8,128)S(1)}, f32[12,1152]{1,0:T(8,128)}, u32[]{:S(2)}) copy-start(f32[12,1152]{1,0:T(8,128)} %param.21) | copy-start | bytes 165892
  617.5 62.9 %copy-start.34 = (f32[48,384]{1,0:T(8,128)S(1)}, f32[48,384]{1,0:T(8,128)}, u32[]{:S(2)}) copy-start(f32[48,384]{1,0:T(8,128)} %param.30) | copy-start | bytes 221188
  626.9 51.9 %copy-start.53 = (f32[12,1152]{1,0:T(8,128)S(1)}, f32[12,1152]{1,0:T(8,128)}, u32[]{:S(2)}) copy-start(f32[12,1152]{1,0:T(8,128)} %param.22) | copy-start | bytes 165892
  628.2 52.2 %copy-start.35 = (f32[48,384]{1,0:T(8,128)S(1)}, f32[48,384]{1,0:T(8,128)}, u32[]{:S(2)}) copy-start(f32[48,384]{1,0:T(8,128)} %reduce-scatter.8.cloned.1.call-done) | copy-start | bytes 221188
  (39 other events, 144.5 us)
Sparse Core Ops, SparseCore 0:
  11.5 57.6 all-gather.7
  72.6 53.0 all-gather.5
  481.3 107.0 reduce-scatter.7
where the time goes:
time: 697 us; the launch traced here: 690 us
  blocking collectives  286 us (41%)
  local copies, waits for them, and re-layouts  142 us (20%)
  matrix products  126 us (18%)
  starting transfers between devices  62 us (9%)
  other arithmetic  51.5 us (7%)
  between operations  20.1 us (3%)
    unnamed x3, blocking collectives  160 us
    unnamed x24, starting transfers between devices  61.9 us
    unnamed x175, local copies, waits for them, and re-layouts  59.2 us
    all_gather x1, blocking collectives, per_device(): lax.all_gather(qkv_low, ('dp', 'fsdp'), axis=0, tiled=True)  43.9 us
    psum x1, blocking collectives, per_device(): clip_norm = jnp.sqrt(lax.psum(squares, ('dp', 'fsdp')))  40.9 us
    all_gather x1, blocking collectives, per_device(): lax.all_gather(proj_low, ('dp', 'fsdp'), axis=0, tiled=True)  40.4 us
    dot_general x1, matrix products, per_device(): jnp.dot(second, up_full, preferred_element_type=jnp.float32) + up_bias  34.8 us
    dot_general x1, matrix products, per_device(): jnp.dot(cotangent, down_back.T, preferred_element_type=jnp.float32)  15 us
  transfers between devices with their start and end apart: 27, of which 1 were waited for; matrix products, arithmetic and copies ran while one was open for 26% of the time, Pallas kernels for 0%

commit v1 on v0

v1 whole, which is shorter than its diff:
```python
import functools
import math

import jax
import jax.numpy as jnp
from jax import lax
from jax.experimental import pallas as pl
from jax.experimental.pallas import tpu as pltpu
from jax.sharding import PartitionSpec as P

D = 384
FF = 1536
HD = 64
STEP = 10
LN_EPS = 1e-05
BETA1 = 0.9
BETA2 = 0.999
ADAM_EPS = 1e-08
DECAY = 0.05
RATES = (0.1, 0.5, 0.1, 0.05)
VECTOR_RATE = 1.0
TB = 256
CH = 256

f32 = jnp.float32
bf16 = jnp.bfloat16
NN = (((1,), (0,)), ((), ()))
NT = (((1,), (1,)), ((), ()))
TN = (((0,), (0,)), ((), ()))
MESH = pl.DeviceIdType.MESH


def dot(a, b, dims=NN):
    return lax.dot_general(a, b, dims, preferred_element_type=f32)


def ln_parts(v):
    centered = v - jnp.mean(v, axis=-1, keepdims=True)
    variance = jnp.mean(centered * centered, axis=-1, keepdims=True)
    return centered, lax.rsqrt(variance + LN_EPS)


def ln_back(grad, xhat, rstd, gain):
    t = grad * gain
    m1 = jnp.mean(t, axis=-1, keepdims=True)
    m2 = jnp.mean(t * xhat, axis=-1, keepdims=True)
    return rstd * (t - m1 - xhat * m2)


def normal_parts(u):
    y = jnp.abs(u) * (2.0**-0.5)
    t = 1.0 / (1.0 + 0.3275911 * y)
    e = jnp.exp(-(y * y))
    tail = t * (
        0.5 * 0.254829592
        + t
        * (
            -0.5 * 0.284496736
            + t * (0.5 * 1.421413741 + t * (-0.5 * 1.453152027 + t * (0.5 * 1.061405429)))
        )
    )
    tail = tail * e
    return jnp.where(u >= 0, 1.0 - tail, tail), e * (1.0 / math.sqrt(2 * math.pi))


def lane_left():
    return lax.broadcasted_iota(jnp.int32, (64, 128), 1) < 64


def two_heads(m, left):
    zero = jnp.zeros_like(m)
    return jnp.concatenate([jnp.where(left, m, zero), jnp.where(left, zero, m)], axis=0)


def diagonal(r, left):
    return jnp.where(left, r[0:64], r[64:128])


def attention_forward(i, mask, qkv, probs, mixed):
    left = lane_left()
    key = lax.broadcasted_iota(jnp.int32, (64, 64), 0)
    query = lax.broadcasted_iota(jnp.int32, (64, 64), 1)
    for c in range(TB // 64):
        cloud = i * (TB // 64) + c
        r = pl.ds(pl.multiple_of(cloud * 64, 64), 64)
        allowed = (key <= query) & ((mask[cloud].T == 1) | (key == query))
        bias = jnp.where(allowed, 0.0, -1e30)
        bias = jnp.concatenate([bias, bias], axis=1)
        for g in range(3):
            q = qkv[r, 128 * g : 128 * g + 128] * jnp.asarray(0.125, bf16)
            k = qkv[r, D + 128 * g : D + 128 * g + 128]
            v = qkv[r, 2 * D + 128 * g : 2 * D + 128 * g + 128]
            s = dot(k, two_heads(q, left), NT) + bias
            e = jnp.exp(s - jnp.max(s, axis=0, keepdims=True))
            p = e * (1.0 / jnp.sum(e, axis=0, keepdims=True))
            probs[r, 128 * g : 128 * g + 128] = p
            o = diagonal(dot(p.astype(bf16), v, TN), left)
            mixed[r, 128 * g : 128 * g + 128] = o.astype(bf16)


def attention_backward(i, qkv, probs, dmix):
    left = lane_left()
    for c in range(TB // 64):
        cloud = i * (TB // 64) + c
        r = pl.ds(pl.multiple_of(cloud * 64, 64), 64)
        for g in range(3):
            sl = slice(128 * g, 128 * g + 128)
            q = qkv[r, 128 * g : 128 * g + 128] * jnp.asarray(0.125, bf16)
            k = qkv[r, D + 128 * g : D + 128 * g + 128]
            v = qkv[r, 2 * D + 128 * g : 2 * D + 128 * g + 128]
            do = two_heads(dmix[r, sl], left)
            p = probs[r, sl]
            dp = dot(v, do, NT)
            ds = (p * (dp - jnp.sum(p * dp, axis=0, keepdims=True))).astype(bf16)
            dv = dot(p.astype(bf16), do)
            dk = dot(ds, two_heads(q, left))
            dq = diagonal(dot(ds, k, TN), left) * 0.125
            qkv[r, 128 * g : 128 * g + 128] = dq.astype(bf16)
            qkv[r, D + 128 * g : D + 128 * g + 128] = dk.astype(bf16)
            qkv[r, 2 * D + 128 * g : 2 * D + 128 * g + 128] = dv.astype(bf16)


def pick_rows(devs, total, shift, step, k, block=None):
    rows = total // devs[2]
    shape = (16 * devs[1], total if block is None else D)
    out = lax.broadcasted_iota(jnp.int32, shape, 0)
    col = lax.broadcasted_iota(jnp.int32, shape, 1)
    if block is not None:
        col = col + D * block
    dev = out >> 4
    i = out - 16 * dev - shift
    ok = (i >= 0) & (i < rows // step) & (col == rows * (dev + devs[0]) + step * i + k)
    return jnp.where(ok, 1.0, 0.0).astype(bf16)


class Layout:
    def __init__(self, n):
        self.n, self.R, self.Rd = n, D // n, FF // n
        R = self.R
        self.fold = 4 * R + 1 <= 16
        groups = [slice(D * k, D * k + D) for k in range(4)]
        if self.fold:
            self.q = [(groups[k], k * R, groups[0]) for k in range(3)]
            self.u = [(groups[k], k * R, groups[0]) for k in range(4)]
            self.p = [(3 * R, 1, 0, groups[0])]
            self.q_sums = [
                (groups[0], [(0, groups[k], k * R, 1, 0) for k in range(3)] + [(1, groups[0], 3 * R, 1, 0)])
            ]
            self.u_sums = [(groups[0], [(groups[k], k * R, 1, 0) for k in range(4)])]
            self.vec_row = 4 * R
            widths = (D, D)
        else:
            self.q = [(slice(0, 3 * D), 0, slice(0, 3 * D))]
            self.u = [(slice(0, FF), 0, slice(0, FF))]
            self.p = [(R, 3, k, groups[k]) for k in range(3)]
            self.q_sums = [
                (groups[k], [(0, groups[k], 0, 1, 0), (1, groups[0], R, 3, k)]) for k in range(3)
            ]
            self.u_sums = [(slice(0, FF), [(slice(0, FF), 0, 1, 0)])]
            self.vec_row = R
            widths = (3 * D, FF)
        tall = self.Rd if self.Rd % 16 == 0 else 16
        self.wide = ((16, widths[0]), (16, widths[1]), (tall, D))

    def p_place(self, i):
        if self.fold:
            return 3 * self.R + i, slice(0, D)
        return self.R + i // 3, slice(D * (i % 3), D * (i % 3) + D)


def layer_kernel(
    dims,
    x_hbm, dy_hbm, mask_hbm, wq_own, wp_own, wu_own, wd_own, vec_own,
    out_hbm, ig_hbm, gq_out, gu_out, gd_out, small_out,
    x, dy, mask, a, qkv, probs, mixed, h1, z_t, du_t,
    gq, gu, gd, wq, wp, wu, wd, vec, bu, vgrid, stage_q, stage_u, stage_d,
    acc_q, acc_p, acc_u, acc_d, dvec, dbu,
    r1q, r1u, r1d, r2q, r2u, r2d, r3q, r3u, r3d,
    small, s1, s2, s3,
    local_sem, ag_send, ag_recv, rs_send, rs_recv, ar_send, ar_recv,
):
    Z, Y, X = dims
    n = Z * Y * X * 2
    lay = Layout(n)
    R, Rd = lay.R, lay.Rd
    T = x.shape[0]
    V = vec_own.shape[1]
    steps = T // TB
    dp = lax.axis_index("dp")
    fs = lax.axis_index("fsdp")
    z, y = dp // Y, dp % Y
    xx, core = fs // 2, fs % 2

    loads = [
        pltpu.make_async_copy(x_hbm, x, local_sem.at[0]),
        pltpu.make_async_copy(mask_hbm, mask, local_sem.at[1]),
        pltpu.make_async_copy(dy_hbm, dy, local_sem.at[2]),
    ]
    for c in loads:
        c.start()

    z_peers = [(k, lax.rem(z + k, Z)) for k in range(1, Z)]
    p_peers = [
        (k, lax.rem(y + k // X, Y), lax.rem(xx + k % X, X)) for k in range(1, X * Y)
    ]
    z_ids = [(zz * Y + y, fs) for _, zz in z_peers]
    p_ids = [(z * Y + yy, pxx * 2 + core) for _, yy, pxx in p_peers]
    c_id = (dp, fs + 1 - 2 * core)
    P1, P2 = len(z_ids), len(p_ids)

    barrier = pltpu.get_barrier_semaphore()
    for dev in z_ids + p_ids + [c_id]:
        pl.semaphore_signal(barrier, inc=1, device_id=dev, device_id_type=MESH)

    stage_q[...] = jnp.zeros_like(stage_q)
    stage_u[...] = jnp.zeros_like(stage_u)
    stage_d[...] = jnp.zeros_like(stage_d)
    for cols, shift, at in lay.q:
        stage_q[shift : shift + R, at] = wq_own[:, cols]
    for i in range(R):
        shift, at = lay.p_place(i)
        stage_q[shift : shift + 1, at] = wp_own[i : i + 1]
    for cols, shift, at in lay.u:
        stage_u[shift : shift + R, at] = wu_own[:, cols]
    stage_u[lay.vec_row : lay.vec_row + 1, 0:V] = vec_own[...]
    stage_d[0:Rd] = wd_own[...]
    gq[z, y, xx, core] = stage_q[...].astype(bf16)
    gu[z, y, xx, core] = stage_u[...].astype(bf16)
    gd[z, y, xx, core] = stage_d[...].astype(bf16)

    pl.semaphore_wait(barrier, P1 + P2 + 1)

    def remote(src, dst, send, recv, dev):
        return pltpu.make_async_remote_copy(
            src_ref=src, dst_ref=dst, send_sem=send, recv_sem=recv, device_id=dev, device_id_type=MESH
        )

    def gather(ch, g, stage):
        if stage == 0:
            return [
                remote(g.at[z, y, xx, core], g.at[z, y, xx, core], ag_send.at[ch, j], ag_recv.at[ch, j], z_ids[j])
                for j in range(P1)
            ]
        if stage == 1:
            return [
                remote(g.at[:, y, xx, core], g.at[:, y, xx, core], ag_send.at[ch, P1 + j], ag_recv.at[ch, P1 + j], p_ids[j])
                for j in range(P2)
            ]
        return [
            remote(g.at[:, :, :, core], g.at[:, :, :, core], ag_send.at[ch, P1 + P2], ag_recv.at[ch, P1 + P2], c_id)
        ]

    bufs = (gq, gu, gd)
    for ch in range(3):
        for c in gather(ch, bufs[ch], 0):
            c.start()
    for stage in (1, 2, 3):
        for ch in range(3):
            for c in gather(ch, bufs[ch], stage - 1):
                c.wait()
            if stage < 3:
                for c in gather(ch, bufs[ch], stage):
                    c.start()

    per_z = 2 * X * Y
    z_group = max(1, min(Z, 32 // per_z))
    groups = [(k, k + z_group, (k * per_z, z_group * per_z, n)) for k in range(0, Z, z_group)]

    def unpack(g, terms, into, cols, via):
        def part(z0, devs):
            flat = g[pl.ds(z0, z_group)].reshape(16 * z_group * per_z, g.shape[-1])
            return sum(
                dot(pick_rows(devs, rows, shift, step, k, *rest), flat[:, at], TN)
                for rows, shift, step, k, at, *rest in terms
            )

        if len(groups) == 1:
            into[:, cols] = part(0, groups[0][2]).astype(bf16)
            return
        via[:, cols] = jnp.zeros((via.shape[0], cols.stop - cols.start), f32)

        @pl.loop(0, len(groups))
        def _(k):
            d0 = k * z_group * per_z
            via[:, cols] += part(k * z_group, (d0, z_group * per_z, n))

        into[:, cols] = via[:, cols].astype(bf16)

    every = slice(0, D)
    for cols, shift, at in lay.q:
        unpack(gq, [(D, shift, 1, 0, at)], wq, cols, acc_q)
    for cols, shift, at in lay.u:
        unpack(gu, [(D, shift, 1, 0, at)], wu, cols, acc_u)
    unpack(gq, [(D,) + p for p in lay.p], wp, every, acc_p)
    if Rd % 16 == 0:
        wd[...] = gd[...].reshape(FF, D)
    else:
        for k in range(FF // D):
            unpack(gd, [(FF, 0, 1, 0, every, k)], wd.at[D * k : D * k + D], every, acc_p)
    for z0, z1, devs in groups:
        first, count, _ = devs
        row = lax.broadcasted_iota(jnp.int32, (count, 16 * count), 0)
        col = lax.broadcasted_iota(jnp.int32, (count, 16 * count), 1)
        pick_vec = jnp.where(col == 16 * row + lay.vec_row, 1.0, 0.0).astype(bf16)
        vgrid[first : first + count] = dot(pick_vec, gu[z0:z1, :, :, :, :, 0:128].reshape(16 * count, 128))
    for d in range(n):
        start, stop = V * d, V * d + V
        while start < stop:
            r0, l0 = start // D, start % D
            size = min(stop - start, D - l0)
            o = start - V * d
            vec[r0 : r0 + 1, l0 : l0 + size] = vgrid[d : d + 1, o : o + size]
            start += size
    for k in range(FF // D):
        bu[:, D * k : D * k + D] = vec[6 + k : 7 + k]

    for r in (acc_q, acc_p, acc_u, acc_d, dvec, dbu):
        r[...] = jnp.zeros_like(r)
    for c in loads:
        c.wait()

    @pl.loop(0, steps)
    def _(i):
        rows = pl.ds(pl.multiple_of(i * TB, TB), TB)
        xv = x[rows, :].astype(f32)
        centered, rstd = ln_parts(xv)
        av = (centered * rstd * vec[0:1] + vec[1:2]).astype(bf16)
        a[rows, :] = av
        qkv[rows, :] = dot(av, wq[...]).astype(bf16)
        attention_forward(i, mask, qkv, probs, mixed)
        h1[rows, :] = xv + (dot(mixed[rows, :], wp[...]) + vec[4:5])

    @pl.loop(0, steps)
    def _(i):
        rows = pl.ds(pl.multiple_of(i * TB, TB), TB)
        h = h1[rows, :]
        centered, rstd = ln_parts(h)
        xhat = centered * rstd
        c = (xhat * vec[2:3] + vec[3:4]).astype(bf16)
        dyv = dy[rows, :]
        for k in range(FF // CH):
            ns = slice(k * CH, (k + 1) * CH)
            u = dot(c, wu[:, ns]) + bu[:, ns]
            dz = dot(dyv, wd[ns, :], NT)
            cdf, density = normal_parts(u)
            zv = (u * cdf).astype(bf16)
            du = (dz * (cdf + u * density)).astype(bf16)
            z_t[:, ns] = zv
            du_t[:, ns] = du
            acc_d[:, ns] += dot(dyv, zv, TN)
            acc_u[:, ns] += dot(c, du, TN)
            dbu[:, ns] += jnp.sum(du.astype(f32), axis=0, keepdims=True)
        dy[rows, :] = (h + (dot(z_t[...], wd[...]) + vec[5:6])).astype(bf16)
        dc = dot(du_t[...], wu[...], NT)
        dyf = dyv.astype(f32)
        dvec[2:3] += jnp.sum(dc * xhat, axis=0, keepdims=True)
        dvec[3:4] += jnp.sum(dc, axis=0, keepdims=True)
        dvec[5:6] += jnp.sum(dyf, axis=0, keepdims=True)
        dh1 = dyf + ln_back(dc, xhat, rstd, vec[2:3])
        h1[rows, :] = dh1
        dr = dh1.astype(bf16)
        dvec[4:5] += jnp.sum(dr.astype(f32), axis=0, keepdims=True)
        acc_p[...] += dot(mixed[rows, :], dr, TN)
        mixed[rows, :] = dot(dr, wp[...], NT).astype(bf16)

    put_out = pltpu.make_async_copy(dy, out_hbm, local_sem.at[3])
    put_out.start()

    @pl.loop(0, steps)
    def _(i):
        rows = pl.ds(pl.multiple_of(i * TB, TB), TB)
        attention_backward(i, qkv, probs, mixed)
        acc_q[...] += dot(a[rows, :], qkv[rows, :], TN)

    @pl.loop(0, steps)
    def _(i):
        rows = pl.ds(pl.multiple_of(i * TB, TB), TB)
        da = dot(qkv[rows, :], wq[...], NT)
        centered, rstd = ln_parts(x[rows, :].astype(f32))
        xhat = centered * rstd
        dvec[0:1] += jnp.sum(da * xhat, axis=0, keepdims=True)
        dvec[1:2] += jnp.sum(da, axis=0, keepdims=True)
        h1[rows, :] = h1[rows, :] + ln_back(da, xhat, rstd, vec[0:1])

    put_ig = pltpu.make_async_copy(h1, ig_hbm, local_sem.at[4])
    put_ig.start()

    def pack(g, at, terms):
        def one(k):
            devs = (k * z_group * per_z, z_group * per_z, n)
            total = sum(
                dot(pick_rows(devs, rows, shift, step, j), source[:, cols].astype(bf16))
                for source, cols, rows, shift, step, j in terms
            )
            shape = (z_group,) + g.shape[1:5] + (total.shape[1],)
            g[pl.ds(k * z_group, z_group), :, :, :, :, at] = total.astype(bf16).reshape(shape)

        if len(groups) == 1:
            one(0)
        else:
            pl.loop(0, len(groups))(one)

    for at, terms in lay.q_sums:
        pack(gq, at, [((acc_q, acc_p)[t[0]], t[1], D) + t[2:] for t in terms])
    for at, terms in lay.u_sums:
        pack(gu, at, [(acc_u, t[0], D) + t[1:] for t in terms])
    if Rd % 16 == 0:
        gd[...] = acc_d[...].astype(bf16).T.reshape(gd.shape)
    else:
        wd[...] = acc_d[...].astype(bf16).T
        pack(gd, slice(0, D), [(wd, slice(0, D), FF, 0, 1, 0)])

    r1 = (r1q, r1u, r1d)
    r2 = (r2q, r2u, r2d)
    r3 = (r3q, r3u, r3d)
    outs = (gq_out, gu_out, gd_out)

    def scatter(ch, stage):
        g = bufs[ch]
        if stage == 0:
            return [remote(g.at[:, :, :, 1 - core], r1[ch], rs_send.at[ch, P1 + P2], rs_recv.at[ch, P1 + P2], c_id)]
        if stage == 1:
            return [
                remote(g.at[:, p_peers[j][1], p_peers[j][2], core], r2[ch].at[j], rs_send.at[ch, P1 + j], rs_recv.at[ch, P1 + j], p_ids[j])
                for j in range(P2)
            ]
        return [
            remote(g.at[z_peers[j][1], y, xx, core], r3[ch].at[j], rs_send.at[ch, j], rs_recv.at[ch, j], z_ids[j])
            for j in range(P1)
        ]

    def add(ch, stage):
        g = bufs[ch]
        if stage == 0:
            for zz in range(Z):
                for yy in range(Y):
                    for cx in range(X):
                        t = g[zz, yy, cx, core].astype(f32) + r1[ch][zz, yy, cx].astype(f32)
                        g[zz, yy, cx, core] = t.astype(bf16)
        elif stage == 1:
            for zz in range(Z):
                t = g[zz, y, xx, core].astype(f32)
                for j in range(P2):
                    t = t + r2[ch][j, zz].astype(f32)
                g[zz, y, xx, core] = t.astype(bf16)
        else:
            t = g[z, y, xx, core].astype(f32)
            for j in range(P1):
                t = t + r3[ch][j].astype(f32)
            outs[ch][...] = t

    for ch in range(3):
        for c in scatter(ch, 0):
            c.start()
    for stage in range(3):
        for ch in range(3):
            for c in scatter(ch, stage):
                c.wait()
            add(ch, stage)
            if stage < 2:
                for c in scatter(ch, stage + 1):
                    c.start()

    squares = jnp.zeros((1, 1), f32)
    for ch in range(3):
        t = outs[ch][...]
        squares = squares + jnp.sum(jnp.sum(t * t, axis=0, keepdims=True), axis=1, keepdims=True)
    small[0] = jnp.zeros((16, D), f32)
    small[0, 0:6] = dvec[0:6]
    for k in range(FF // D):
        small[0, 6 + k : 7 + k] = dbu[:, D * k : D * k + D]
    small[0, 10:11] = jnp.broadcast_to(squares, (1, D))

    def spread(stage):
        if stage == 0:
            return [remote(small.at[0], s1.at[j], ar_send.at[j], ar_recv.at[j], z_ids[j]) for j in range(P1)]
        if stage == 1:
            return [remote(small.at[1], s2.at[j], ar_send.at[P1 + j], ar_recv.at[P1 + j], p_ids[j]) for j in range(P2)]
        return [remote(small.at[2], s3.at[0], ar_send.at[P1 + P2], ar_recv.at[P1 + P2], c_id)]

    received = (s1, s2, s3)
    for stage in range(3):
        copies = spread(stage)
        for c in copies:
            c.start()
        for c in copies:
            c.wait()
        t = small[stage]
        for j in range(len(copies)):
            t = t + received[stage][j]
        if stage < 2:
            small[stage + 1] = t
        else:
            small_out[...] = t
    put_out.wait()
    put_ig.wait()


def layer_call(dims, x, dy, masks, wq, wp, wu, wd, vec):
    Z, Y, X = dims
    n = Z * Y * X * 2
    T = x.shape[0]
    S = jax.ShapeDtypeStruct
    V = pltpu.VMEM
    vm = pl.BlockSpec(memory_space=pltpu.VMEM)
    hbm = pl.BlockSpec(memory_space=pl.ANY)
    peers = (Z - 1) + (X * Y - 1) + 1
    wide = Layout(n).wide
    scratch = [
        V((T, D), bf16), V((T, D), bf16), V(masks.shape, jnp.int32),
        V((T, D), bf16), V((T, 3 * D), bf16), V((T, D), f32), V((T, D), bf16), V((T, D), f32),
        V((TB, FF), bf16), V((TB, FF), bf16),
    ]
    scratch += [V((Z, Y, X, 2) + w, bf16) for w in wide]
    scratch += [V((D, 3 * D), bf16), V((D, D), bf16), V((D, FF), bf16), V((FF, D), bf16)]
    scratch += [V((16, D), f32), V((1, FF), f32), V((n, 128), f32)]
    scratch += [V(w, f32) for w in wide]
    scratch += [V((D, 3 * D), f32), V((D, D), f32), V((D, FF), f32), V((D, FF), f32), V((8, D), f32), V((1, FF), f32)]
    scratch += [V((Z, Y, X) + w, bf16) for w in wide]
    scratch += [V((X * Y - 1, Z) + w, bf16) for w in wide]
    scratch += [V((Z - 1,) + w, bf16) for w in wide]
    scratch += [V((3, 16, D), f32), V((Z - 1, 16, D), f32), V((X * Y - 1, 16, D), f32), V((1, 16, D), f32)]
    dma = pltpu.SemaphoreType.DMA
    scratch += [dma((5,)), dma((3, peers)), dma((3, peers)), dma((3, peers)), dma((3, peers)), dma((peers,)), dma((peers,))]
    return pl.pallas_call(
        functools.partial(layer_kernel, dims),
        out_shape=[S((T, D), bf16), S((T, D), f32)] + [S(w, f32) for w in wide] + [S((16, D), f32)],
        in_specs=[hbm] * 3 + [vm] * 5,
        out_specs=[hbm] * 2 + [vm] * 4,
        scratch_shapes=scratch,
        compiler_params=pltpu.CompilerParams(
            collective_id=0, has_side_effects=True, vmem_limit_bytes=60 * 1024 * 1024
        ),
        name="layer",
    )(x, dy, masks, wq, wp, wu, wd, vec)


def adam_step(w, m, r, g, rate, decay):
    m_new = BETA1 * m + (1.0 - BETA1) * g
    r_new = BETA2 * r + (1.0 - BETA2) * g * g
    m_hat = m_new / (1.0 - BETA1**STEP)
    r_hat = r_new / (1.0 - BETA2**STEP)
    return w - rate * (m_hat / (jnp.sqrt(r_hat) + ADAM_EPS) + decay * w), m_new, r_new


def adam_kernel(n, *refs):
    small, gq, gu, gd = refs[0:4]
    state = refs[4:19]
    out_in, ig_in = refs[19:21]
    out_ref, ig_ref, norm = refs[21:24]
    new = refs[24:39]
    sem = refs[39]
    out_v, ig_v = refs[40:42]
    lay = Layout(n)
    R, Rd, V = lay.R, lay.Rd, state[12].shape[1]
    T = out_v.shape[0]
    parts = [pl.ds(k * (T // 4), T // 4) for k in range(4)]
    loads = [pltpu.make_async_copy(out_in.at[r], out_v.at[r], sem.at[k]) for k, r in enumerate(parts)]
    loads += [pltpu.make_async_copy(ig_in.at[r], ig_v.at[r], sem.at[4 + k]) for k, r in enumerate(parts)]
    stores = [pltpu.make_async_copy(out_v.at[r], out_ref.at[r], sem.at[8 + k]) for k, r in enumerate(parts)]
    stores += [pltpu.make_async_copy(ig_v.at[r], ig_ref.at[r], sem.at[12 + k]) for k, r in enumerate(parts)]
    for c in loads:
        c.start()
    for c, d in zip(loads, stores):
        c.wait()
        d.start()
    vecs = small[0:10]
    squares = jnp.sum(jnp.sum(vecs * vecs, axis=0, keepdims=True), axis=1, keepdims=True) + small[10:11, 0:1]
    clip = jnp.sqrt(squares)
    norm[...] = clip
    factor = 1.0 / clip

    def step(k, rows, cols, g, rate, decay):
        w, m, r = (ref[rows, cols] for ref in state[3 * k : 3 * k + 3])
        for ref, value in zip(new[3 * k : 3 * k + 3], adam_step(w, m, r, g * factor, rate, decay)):
            ref[rows, cols] = value

    every = slice(0, D)
    for cols, shift, at in lay.q:
        step(0, slice(0, R), cols, gq[shift : shift + R, at], RATES[0], DECAY)
    for i in range(R):
        shift, at = lay.p_place(i)
        step(1, slice(i, i + 1), every, gq[shift : shift + 1, at], RATES[1], DECAY)
    for cols, shift, at in lay.u:
        step(2, slice(0, R), cols, gu[shift : shift + R, at], RATES[2], DECAY)
    step(3, slice(0, Rd), every, gd[0:Rd], RATES[3], DECAY)
    me = lax.axis_index("dp") * (n // lax.axis_size("dp")) + lax.axis_index("fsdp")
    start = me * V
    row, lane = start // D, lax.rem(start, D)
    two = jnp.concatenate([small[pl.ds(row, 1), :], small[pl.ds(row + 1, 1), :]], axis=1)
    two = pltpu.roll(jnp.broadcast_to(two, (8, 2 * D)), 2 * D - lane, 1)
    step(4, slice(0, 1), slice(0, V), two[0:1, 0:V], VECTOR_RATE, 0.0)
    for c in stores:
        c.wait()


def adam_call(n, small, gq, gu, gd, state, out, ig):
    vm = pl.BlockSpec(memory_space=pltpu.VMEM)
    hbm = pl.BlockSpec(memory_space=pl.ANY)
    S = jax.ShapeDtypeStruct
    return pl.pallas_call(
        functools.partial(adam_kernel, n),
        out_shape=[S(out.shape, out.dtype), S(ig.shape, ig.dtype), S((1, 1), f32)] + [S(s.shape, f32) for s in state],
        in_specs=[vm] * 19 + [hbm] * 2,
        out_specs=[hbm] * 2 + [vm] * 16,
        scratch_shapes=[pltpu.SemaphoreType.DMA((16,)), pltpu.VMEM(out.shape, out.dtype), pltpu.VMEM(ig.shape, ig.dtype)],
        name="adam",
    )(small, gq, gu, gd, *state, out, ig)


def solution(mesh):
    n_dp, n_fs = mesh.shape["dp"], mesh.shape["fsdp"]
    X = n_fs // 2
    Y = X if n_dp % X == 0 else 1
    dims = (n_dp // Y, Y, X)
    n = n_dp * n_fs

    def per_device(x, dy, masks, *state):
        state = list(state)
        flat = [s.shape for s in state[12:15]]
        state[12:15] = [s.reshape(1, -1) for s in state[12:15]]
        out, ig, gq, gu, gd, small = layer_call(
            dims, x, dy, masks, state[0], state[3], state[6], state[9], state[12]
        )
        res = adam_call(n, small, gq, gu, gd, state, out, ig)
        new = list(res[3:])
        new[12:15] = [v.reshape(f) for v, f in zip(new[12:15], flat)]
        return (res[0], res[1], res[2].reshape(()), *new)

    rows = P(("dp", "fsdp"), None)
    line = P(("dp", "fsdp"))
    placed = (rows, rows, P(("dp", "fsdp"), None, None)) + (rows,) * 12 + (line,) * 3
    given = (rows, rows, P()) + (rows,) * 12 + (line,) * 3
    return jax.shard_map(per_device, mesh=mesh, in_specs=placed, out_specs=given, check_vma=False)
```

time: 697 us -> 191 us (0.27)
  blocking collectives: 286 us -> 0 us
  Pallas kernels: 0 us -> 190 us
  local copies, waits for them, and re-layouts: 142 us -> 0 us
  matrix products: 126 us -> 0 us
  starting transfers between devices: 62 us -> 0 us
  other arithmetic: 51.5 us -> 0 us
  between operations: 20.1 us -> 0.82 us
    pallas_call x0 -> x2, Pallas kernels: none -> 190 us  [the longest x1 183 us: layer_call(): pl.pallas_call(functools.partial(layer_kernel, dims), out_shape=[S((T, D)...]
    unnamed x3 -> x0, blocking collectives: 160 us -> none
    dot_general x18 -> x0, matrix products: 126 us -> none  [the longest x1 34.8 us: per_device(): jnp.dot(second, up_full, preferred_element_type=jnp.float32) + up_bias]
    all_gather x2 -> x0, blocking collectives: 84.3 us -> none  [the longest x1 43.9 us: per_device(): lax.all_gather(qkv_low, ('dp', 'fsdp'), axis=0, tiled=True)]
    unnamed x24 -> x0, starting transfers between devices: 61.9 us -> none
    unnamed x175 -> x0, local copies, waits for them, and re-layouts: 59.2 us -> none
    psum x1 -> x0, blocking collectives: 40.9 us -> none  [per_device(): clip_norm = jnp.sqrt(lax.psum(squares, ('dp', 'fsdp')))]
    convert_element_type x4 -> x0, local copies, waits for them, and re-layouts: 28.9 us -> none  [the longest x1 13.9 us: per_device(): grad_packed = jnp.stack((grad_queries, grad_keys, grad_values), axis=2).r...]
  transfers between devices with their start and end apart: 27 -> 0, of which waited for: 1 -> 0; matrix products, arithmetic and copies ran while one was open for 26% -> 0% of each run, Pallas kernels for 0% -> 0%
where the time goes in v1:
time: 191 us
  Pallas kernels  190 us (99%)
    pallas_call x1, Pallas kernels, layer_call(): pl.pallas_call(functools.partial(layer_kernel, dims), out_shape=[S((T, D)...  183 us
    pallas_call x1, Pallas kernels, adam_call(): pl.pallas_call(functools.partial(adam_kernel, n), out_shape=[S(out.shape,...  6.69 us

profile of v1, /device:TPU:0, one launch (start us, length us, event | category | flops | bytes accessed | tf_op | source)
XLA Modules:
  0.0 190.5 jit_solution(9833331982487842331)
XLA Ops:
  0.7 183.0 %layer.1 = (bf16[2048,384]{1,0:T(8,128)(2,1)}, f32[2048,384]{1,0:T(8,128)}, f32[16,1152]{1,0:T(8,128)}, f32[16,1536]{1,0:T(8,128)}, f32[48,384]{1,0:T(8,128)}, /*index=5*/f32[16,384]{1,0:T(8,128)}) custom-call(bf16[2048,384]{1,0:T(8,128)(2,1)} %x_hbm.1, bf16[2048,384]{1,0:T(8,128)(2,1)} %dy_hbm.1, s32[32,64,64]{2,1,0:T(8,128)} %mask_hbm.1, ...), custom_call_target="tpu_custom_call" | custom-call | tf_op jit(solution)/shard_map/layer/pallas_call | solution.py:525
  183.7 6.7 %adam.1 = (bf16[2048,384]{1,0:T(8,128)(2,1)}, f32[2048,384]{1,0:T(8,128)}, f32[1,1]{1,0:T(1,128)}, f32[12,1152]{1,0:T(8,128)}, f32[12,1152]{1,0:T(8,128)}, /*ind...) custom-call(f32[16,384]{1,0:T(8,128)} %get-tuple-element.42.refs_0_,, ...), custom_call_target="tpu_custom_call" | custom-call | tf_op jit(solution)/shard_map/adam/pallas_call | solution.py:601

commit v2 on v1

v2 whole, which is shorter than its diff:
```python
import functools
import math

import jax
import jax.numpy as jnp
from jax import lax
from jax.experimental import pallas as pl
from jax.experimental.pallas import tpu as pltpu
from jax.sharding import PartitionSpec as P

D = 384
FF = 1536
HD = 64
STEP = 10
NORM_EPS = 1e-05
BETA1 = 0.9
BETA2 = 0.999
ADAM_EPS = 1e-08
DECAY = 0.05
RATES = (0.1, 0.5, 0.1, 0.05)
VECTOR_RATE = 1.0
TB = 512
TA = 1024
CH = 512

f32 = jnp.float32
bf16 = jnp.bfloat16
NN = (((1,), (0,)), ((), ()))
NT = (((1,), (1,)), ((), ()))
TN = (((0,), (0,)), ((), ()))
MESH = pl.DeviceIdType.MESH


def dot(a, b, dims=NN):
    return lax.dot_general(a, b, dims, preferred_element_type=f32)


def ln_parts(v):
    centered = v - jnp.mean(v, axis=-1, keepdims=True)
    variance = jnp.mean(centered * centered, axis=-1, keepdims=True)
    return centered, lax.rsqrt(variance + NORM_EPS)


def ln_back(grad, xhat, rstd, gain):
    t = grad * gain
    m1 = jnp.mean(t, axis=-1, keepdims=True)
    m2 = jnp.mean(t * xhat, axis=-1, keepdims=True)
    return rstd * (t - m1 - xhat * m2)


def gelu_parts(u):
    cdf = 0.5 + 0.5 * lax.erf(u * (2.0**-0.5))
    density = jnp.exp2(u * u * (-0.5 * math.log2(math.e))) * (1.0 / math.sqrt(2 * math.pi))
    return u * cdf, cdf + u * density


def lane_left():
    return lax.broadcasted_iota(jnp.int32, (64, 128), 1) < 64


def two_heads(m, left):
    zero = jnp.zeros_like(m)
    return jnp.concatenate([jnp.where(left, m, zero), jnp.where(left, zero, m)], axis=0)


def diagonal(r, left):
    return jnp.where(left, r[0:64], r[64:128])


def attention_forward(i, mask, qkv, probs, mixed):
    left = lane_left()
    key = lax.broadcasted_iota(jnp.int32, (64, 64), 0)
    query = lax.broadcasted_iota(jnp.int32, (64, 64), 1)
    clouds = TB // 64
    rows = [pl.ds(pl.multiple_of(i * TB + 64 * c, 64), 64) for c in range(clouds)]
    units = [(c, g) for c in range(clouds) for g in range(3)]
    bias = []
    for c in range(clouds):
        allowed = (key <= query) & ((mask[i * clouds + c].T == 1) | (key == query))
        b = jnp.where(allowed, 0.0, -1e30)
        bias.append(jnp.concatenate([b, b], axis=1))
    held = {}
    for c, g in units:
        q = qkv[rows[c], D * g : D * g + 128] * jnp.asarray(0.125, bf16)
        k = qkv[rows[c], D * g + 128 : D * g + 256]
        held[c, g] = dot(k, two_heads(q, left), NT) + bias[c]
    for c, g in units:
        s = held[c, g]
        e = jnp.exp(s - jnp.max(s, axis=0, keepdims=True))
        p = e * (1.0 / jnp.sum(e, axis=0, keepdims=True))
        probs[rows[c], 128 * g : 128 * g + 128] = p
        held[c, g] = p.astype(bf16)
    for c, g in units:
        v = qkv[rows[c], D * g + 256 : D * g + 384]
        mixed[rows[c], 128 * g : 128 * g + 128] = diagonal(dot(held[c, g], v, TN), left).astype(bf16)


def attention_backward(i, g, qkv, probs, dmix, dqkv):
    left = lane_left()
    across = slice(128 * g, 128 * g + 128)
    rows = [pl.ds(pl.multiple_of(i * TA + 64 * c, 64), 64) for c in range(TA // 64)]
    held = []
    for r in rows:
        v = qkv[r, D * g + 256 : D * g + 384]
        held.append(dot(v, two_heads(dmix[r, across], left), NT))
    for c, r in enumerate(rows):
        p, dp = probs[r, across], held[c]
        held[c] = (p * (dp - jnp.sum(p * dp, axis=0, keepdims=True))).astype(bf16)
    for ds, r in zip(held, rows):
        q = qkv[r, D * g : D * g + 128] * jnp.asarray(0.125, bf16)
        k = qkv[r, D * g + 128 : D * g + 256]
        dv = dot(probs[r, across].astype(bf16), two_heads(dmix[r, across], left))
        dk = dot(ds, two_heads(q, left))
        dq = diagonal(dot(ds, k, TN), left) * 0.125
        dqkv[r, D * g : D * g + 128] = dq.astype(bf16)
        dqkv[r, D * g + 128 : D * g + 256] = dk.astype(bf16)
        dqkv[r, D * g + 256 : D * g + 384] = dv.astype(bf16)


def pick_rows(devs, total, shift, step, k, block=None):
    rows = total // devs[2]
    shape = (16 * devs[1], total if block is None else D)
    out = lax.broadcasted_iota(jnp.int32, shape, 0)
    col = lax.broadcasted_iota(jnp.int32, shape, 1)
    if block is not None:
        col = col + D * block
    dev = out >> 4
    i = out - 16 * dev - shift
    ok = (i >= 0) & (i < rows // step) & (col == rows * (dev + devs[0]) + step * i + k)
    return jnp.where(ok, 1.0, 0.0).astype(bf16)


class Layout:
    def __init__(self, n):
        self.n, self.R, self.Rd = n, D // n, FF // n
        R = self.R
        self.fold = 4 * R <= 16
        groups = [slice(D * k, D * k + D) for k in range(4)]
        if self.fold:
            self.u = [(groups[k], k * R, groups[0]) for k in range(4)]
            self.u_sums = [(groups[0], [(groups[k], k * R) for k in range(4)])]
        else:
            self.u = [(slice(0, FF), 0, slice(0, FF))]
            self.u_sums = [(slice(0, FF), [(slice(0, FF), 0)])]
        self.straight = self.Rd % 16 == 0
        self.blocks = ((16, D),) * 3 + ((16, D if self.fold else FF), (self.Rd if self.straight else 16, D))


def layer_kernel(dims, *refs):
    Z, Y, X = dims
    n = Z * Y * X * 2
    lay = Layout(n)
    R, Rd = lay.R, lay.Rd
    it = iter(refs)

    def take(count=None):
        return next(it) if count is None else [next(it) for _ in range(count)]

    x_hbm, dy_hbm, mask_hbm, wq_own, wp_own, wu_own, wd_own, vec_own = take(8)
    out_hbm, ig_hbm, gq_out, gu_out, gd_out, small_out, norm_out = take(7)
    x, dy, mask, a, qkv, probs, mixed, h1, dh1, c_all, z_all, du_all = take(12)
    bufs = take(6)
    wq, wp, wu, wd, vec, bu, vgrid, sel, tmp_d, tmp_q = take(10)
    stage = take(6)
    acc_p, dvec, dbu = take(3)
    r1, r2, r3 = take(5), take(5), take(5)
    small, s1, s2, s3, sq, sq_in = take(6)
    local_sem, ag_send, ag_recv, rs_send, rs_recv, ar_send, ar_recv, sq_send, sq_recv = take(9)
    outs = [gq_out.at[0], gq_out.at[1], gq_out.at[2], gu_out, gd_out]

    T = x.shape[0]
    V = vec_own.shape[1]
    steps = T // TB
    dp = lax.axis_index("dp")
    fs = lax.axis_index("fsdp")
    z, y = dp // Y, lax.rem(dp, Y)
    xx, core = fs // 2, lax.rem(fs, 2)

    loads = [
        pltpu.make_async_copy(x_hbm, x, local_sem.at[0]),
        pltpu.make_async_copy(mask_hbm, mask, local_sem.at[1]),
        pltpu.make_async_copy(dy_hbm, dy, local_sem.at[2]),
    ]
    for c in loads:
        c.start()

    chips = [
        (lax.rem(z + k // (X * Y), Z), lax.rem(y + k // X % Y, Y), lax.rem(xx + k % X, X)) for k in range(1, Z * Y * X)
    ]
    chip_ids = [(c[0] * Y + c[1], c[2] * 2 + core) for c in chips]
    in_z = [k * X * Y - 1 for k in range(1, Z)]
    in_p = list(range(X * Y - 1))
    z_peers, z_ids = [chips[k] for k in in_z], [chip_ids[k] for k in in_z]
    p_peers, p_ids = [chips[k] for k in in_p], [chip_ids[k] for k in in_p]
    c_id = (dp, fs + 1 - 2 * core)
    P1, P2 = len(z_ids), len(p_ids)

    barrier = pltpu.get_barrier_semaphore()
    for dev in chip_ids + [c_id]:
        pl.semaphore_signal(barrier, inc=1, device_id=dev, device_id_type=MESH)

    for s in stage:
        s[...] = jnp.zeros_like(s)
    for g in range(3):
        for j in range(3):
            stage[g][0:R, 128 * j : 128 * j + 128] = wq_own[:, D * j + 128 * g : D * j + 128 * g + 128]
    for i in range(R):
        stage[i % 3][R + i // 3 : R + i // 3 + 1] = wp_own[i : i + 1]
    for cols, shift, at in lay.u:
        stage[3][shift : shift + R, at] = wu_own[:, cols]
    stage[5][0:1, 0:V] = vec_own[...]
    stage[4][0:Rd] = wd_own[...]
    for g, s in zip(bufs, stage):
        g[z, y, xx, core] = s[...].astype(bf16)

    pl.semaphore_wait(barrier, len(chip_ids) + 1)

    def remote(src, dst, send, recv, dev):
        return pltpu.make_async_remote_copy(
            src_ref=src, dst_ref=dst, send_sem=send, recv_sem=recv, device_id=dev, device_id_type=MESH
        )

    def gather(ch, stage):
        g = bufs[ch]
        send, recv = ag_send.at[ch], ag_recv.at[ch]
        if stage == 0:
            own = g.at[z, y, xx, core]
            return [remote(own, own, send.at[j], recv.at[j], z_ids[j]) for j in range(P1)]
        if stage == 1:
            own = g.at[:, y, xx, core]
            return [remote(own, own, send.at[P1 + j], recv.at[P1 + j], p_ids[j]) for j in range(P2)]
        own = g.at[:, :, :, core]
        return [remote(own, own, send.at[P1 + P2], recv.at[P1 + P2], c_id)]

    def gather_step(ch, stage):
        if stage > 0:
            for c in gather(ch, stage - 1):
                c.wait()
        if stage < 3:
            for c in gather(ch, stage):
                c.start()

    def scatter(ch, stage):
        g = bufs[ch]
        send, recv = rs_send.at[ch], rs_recv.at[ch]
        if stage == 0:
            return [remote(g.at[:, :, :, 1 - core], r1[ch], send.at[P1 + P2], recv.at[P1 + P2], c_id)]
        if stage == 1:
            return [
                remote(g.at[:, p_peers[j][1], p_peers[j][2], core], r2[ch].at[j], send.at[P1 + j], recv.at[P1 + j], p_ids[j])
                for j in range(P2)
            ]
        return [
            remote(g.at[z_peers[j][0], y, xx, core], r3[ch].at[j], send.at[j], recv.at[j], z_ids[j]) for j in range(P1)
        ]

    def scatter_step(ch, stage):
        g = bufs[ch]
        if stage > 0:
            for c in scatter(ch, stage - 1):
                c.wait()
        if stage == 1:
            for zz in range(Z):
                for yy in range(Y):
                    for cx in range(X):
                        t = g[zz, yy, cx, core].astype(f32) + r1[ch][zz, yy, cx].astype(f32)
                        g[zz, yy, cx, core] = t.astype(bf16)
        elif stage == 2:
            for zz in range(Z):
                t = g[zz, y, xx, core].astype(f32)
                for j in range(P2):
                    t = t + r2[ch][j, zz].astype(f32)
                g[zz, y, xx, core] = t.astype(bf16)
        elif stage == 3:
            t = g[z, y, xx, core].astype(f32)
            for j in range(P1):
                t = t + r3[ch][j].astype(f32)
            outs[ch][...] = t
        if stage < 3:
            for c in scatter(ch, stage):
                c.start()

    per_z = 2 * X * Y
    z_group = max(1, min(Z, 32 // per_z))
    count = z_group * per_z
    n_groups = Z // z_group
    SEL = {(0, 1, 0): 0, (R, 3, 0): 1, (R, 3, 1): 2, (R, 3, 2): 3}

    def pick(k, rows, shift, step, first, block=None):
        if n_groups == 1 and (shift, step, first) in SEL and rows == D:
            return sel[SEL[shift, step, first]]
        return pick_rows((k * count, count, n), rows, shift, step, first, block)

    def by_groups(f):
        if n_groups == 1:
            f(0)
        else:
            pl.loop(0, n_groups)(f)

    def unpack(into, cols, terms):
        def part(k):
            total = None
            for g, at, rows, shift, step, first, block in terms:
                flat = g[pl.ds(k * z_group, z_group), :, :, :, :, at].reshape(16 * count, at.stop - at.start)
                t = dot(pick(k, rows, shift, step, first, block), flat, TN)
                total = t if total is None else total + t
            if n_groups == 1:
                into[:, cols] = total.astype(bf16)
            else:
                into[:, cols] = (into[:, cols].astype(f32) + total).astype(bf16)

        if n_groups > 1:
            into[:, cols] = jnp.zeros((into.shape[0], cols.stop - cols.start), bf16)
        by_groups(part)

    def pack(g, at, terms):
        def one(k):
            total = None
            for source, cols, rows, shift, step, first in terms:
                t = dot(pick(k, rows, shift, step, first), source[:, cols])
                total = t if total is None else total + t
            shape = (z_group,) + g.shape[1:5] + (total.shape[1],)
            g[pl.ds(k * z_group, z_group), :, :, :, :, at] = total.astype(bf16).reshape(shape)

        by_groups(one)

    every = slice(0, D)

    for ch in (5, 0, 1, 2):
        gather_step(ch, 0)
    if n_groups == 1:
        for (shift, step, first), k in SEL.items():
            sel[k] = pick_rows((0, n, n), D, shift, step, first)
    for r in (acc_p, dvec, dbu):
        r[...] = jnp.zeros_like(r)
    for c in loads:
        c.wait()
    for ch in (5, 0, 1, 2):
        gather_step(ch, 1)
    gather_step(3, 0)
    dvec[5:6] = jnp.sum(dy[...].astype(f32), axis=0, keepdims=True)
    for ch in (5, 0, 1, 2):
        gather_step(ch, 2)
    gather_step(3, 1)
    gather_step(4, 0)
    for ch in range(3):
        gather_step(ch, 3)
        unpack(wq, slice(D * ch, D * ch + D), [(bufs[ch], every, D, 0, 1, 0, None)])
    unpack(wp, every, [(bufs[k], every, D, R, 3, k, None) for k in range(3)])

    gather_step(5, 3)
    for k in range(n_groups):
        row = lax.broadcasted_iota(jnp.int32, (count, 16 * count), 0)
        col = lax.broadcasted_iota(jnp.int32, (count, 16 * count), 1)
        pick_vec = jnp.where(col == 16 * row, 1.0, 0.0).astype(bf16)
        flat = bufs[5][k * z_group : (k + 1) * z_group].reshape(16 * count, 128)
        vgrid[k * count : (k + 1) * count] = dot(pick_vec, flat)
    for d in range(n):
        start, stop = V * d, V * d + V
        while start < stop:
            r0, l0 = start // D, start % D
            size = min(stop - start, D - l0)
            o = start - V * d
            vec[r0 : r0 + 1, l0 : l0 + size] = vgrid[d : d + 1, o : o + size]
            start += size
    for k in range(FF // D):
        bu[:, D * k : D * k + D] = vec[6 + k : 7 + k]

    @pl.loop(0, steps)
    def _(i):
        @pl.when(i == 1)
        def _():
            gather_step(3, 2)
            gather_step(4, 1)

        rows = pl.ds(pl.multiple_of(i * TB, TB), TB)
        xv = x[rows, :].astype(f32)
        centered, rstd = ln_parts(xv)
        av = (centered * rstd * vec[0:1] + vec[1:2]).astype(bf16)
        a[rows, :] = av
        qkv[rows, :] = dot(av, wq[...]).astype(bf16)
        attention_forward(i, mask, qkv, probs, mixed)
        h1[rows, :] = xv + (dot(mixed[rows, :], wp[...]) + vec[4:5])

    gather_step(4, 2)
    gather_step(3, 3)
    for cols, shift, at in lay.u:
        unpack(wu, cols, [(bufs[3], at, D, shift, 1, 0, None)])
    gather_step(4, 3)
    if lay.straight:
        wd[...] = bufs[4][...].reshape(FF, D)
    else:
        for k in range(FF // D):
            unpack(wd.at[D * k : D * k + D], every, [(bufs[4], every, FF, 0, 1, 0, k)])

    @pl.loop(0, steps)
    def _(i):
        rows = pl.ds(pl.multiple_of(i * TB, TB), TB)
        centered, rstd = ln_parts(h1[rows, :])
        c = (centered * rstd * vec[2:3] + vec[3:4]).astype(bf16)
        c_all[rows, :] = c
        dyv = dy[rows, :]
        cuts = [slice(k * CH, (k + 1) * CH) for k in range(FF // CH)]
        ahead = dot(c, wu[:, cuts[0]]), dot(dyv, wd[cuts[0], :], NT)
        for k, ns in enumerate(cuts):
            u, dz = ahead
            if k + 1 < len(cuts):
                ahead = dot(c, wu[:, cuts[k + 1]]), dot(dyv, wd[cuts[k + 1], :], NT)
            zv, slope = gelu_parts(u + bu[:, ns])
            z_all[rows, ns] = zv.astype(bf16)
            du = (dz * slope).astype(bf16)
            du_all[rows, ns] = du
            dbu[:, ns] += jnp.sum(du.astype(f32), axis=0, keepdims=True)

    if lay.straight:
        bufs[4][...] = dot(dy[...], z_all[...], TN).astype(bf16).T.reshape(bufs[4].shape)
    else:
        tmp_d[...] = dot(dy[...], z_all[...], TN).astype(bf16).T
        pack(bufs[4], every, [(tmp_d, every, FF, 0, 1, 0)])
    scatter_step(4, 0)

    dmix = mixed

    @pl.loop(0, steps)
    def _(i):
        rows = pl.ds(pl.multiple_of(i * TB, TB), TB)
        dc = dot(du_all[rows, :], wu[...], NT)
        centered, rstd = ln_parts(h1[rows, :])
        xhat = centered * rstd
        dvec[2:3] += jnp.sum(dc * xhat, axis=0, keepdims=True)
        dvec[3:4] += jnp.sum(dc, axis=0, keepdims=True)
        d1 = dy[rows, :].astype(f32) + ln_back(dc, xhat, rstd, vec[2:3])
        dh1[rows, :] = d1
        dr = d1.astype(bf16)
        dvec[4:5] += jnp.sum(dr.astype(f32), axis=0, keepdims=True)
        acc_p[...] += dot(mixed[rows, :], dr, TN)
        dmix[rows, :] = dot(dr, wp[...], NT).astype(bf16)

    scatter_step(4, 1)
    wu[...] = dot(c_all[...], du_all[...], TN).astype(bf16)
    for at, terms in lay.u_sums:
        pack(bufs[3], at, [(wu, cols, D, shift, 1, 0) for cols, shift in terms])
    scatter_step(3, 0)
    wp[...] = acc_p[...].astype(bf16)

    dqkv = du_all

    for g in range(3):
        @pl.loop(0, T // TA)
        def _(i):
            attention_backward(i, g, qkv, probs, dmix, dqkv)

        if g == 0:
            scatter_step(3, 1)
        if g == 1:
            scatter_step(0, 1)
            scatter_step(4, 2)
        if g == 2:
            scatter_step(1, 1)
        tmp_q[...] = dot(a[...], dqkv[:, D * g : D * g + D], TN).astype(bf16)
        pack(bufs[g], every, [(tmp_q, every, D, 0, 1, 0), (wp, every, D, R, 3, g)])
        scatter_step(g, 0)

    @pl.loop(0, steps)
    def _(i):
        rows = pl.ds(pl.multiple_of(i * TB, TB), TB)
        da = dot(dqkv[rows, 0 : 3 * D], wq[...], NT)
        centered, rstd = ln_parts(x[rows, :].astype(f32))
        xhat = centered * rstd
        dvec[0:1] += jnp.sum(da * xhat, axis=0, keepdims=True)
        dvec[1:2] += jnp.sum(da, axis=0, keepdims=True)
        dh1[rows, :] = dh1[rows, :] + ln_back(da, xhat, rstd, vec[0:1])

    put_ig = pltpu.make_async_copy(dh1, ig_hbm, local_sem.at[4])
    put_ig.start()
    scatter_step(2, 1)
    scatter_step(3, 2)

    small[0] = jnp.zeros((16, D), f32)
    small[0, 0:6] = dvec[0:6]
    for k in range(FF // D):
        small[0, 6 + k : 7 + k] = dbu[:, D * k : D * k + D]
    received = (s1, s2, s3)

    def spread(stage):
        if stage == 0:
            return [remote(small.at[0], s1.at[j], ar_send.at[j], ar_recv.at[j], z_ids[j]) for j in range(P1)]
        if stage == 1:
            return [remote(small.at[1], s2.at[j], ar_send.at[P1 + j], ar_recv.at[P1 + j], p_ids[j]) for j in range(P2)]
        return [remote(small.at[2], s3.at[0], ar_send.at[P1 + P2], ar_recv.at[P1 + P2], c_id)]

    def spread_step(stage):
        if stage > 0:
            copies = spread(stage - 1)
            for c in copies:
                c.wait()
            t = small[stage - 1]
            for j in range(len(copies)):
                t = t + received[stage - 1][j]
            if stage < 3:
                small[stage] = t
            else:
                small_out[...] = t
        if stage < 3:
            for c in spread(stage):
                c.start()

    spread_step(0)

    @pl.loop(0, steps)
    def _(i):
        rows = pl.ds(pl.multiple_of(i * TB, TB), TB)
        dy[rows, :] = (h1[rows, :] + (dot(z_all[rows, :], wd[...]) + vec[5:6])).astype(bf16)

    put_out = pltpu.make_async_copy(dy, out_hbm, local_sem.at[3])
    put_out.start()

    scatter_step(0, 2)
    spread_step(1)
    scatter_step(1, 2)
    scatter_step(4, 3)
    scatter_step(2, 2)
    spread_step(2)
    scatter_step(3, 3)
    spread_step(3)
    for ch in range(3):
        scatter_step(ch, 3)

    squares = jnp.zeros((1, 1), f32)
    for ref in outs:
        t = ref[...]
        squares = squares + jnp.sum(jnp.sum(t * t, axis=0, keepdims=True), axis=1, keepdims=True)
    sq[0] = jnp.broadcast_to(squares, (8, 128))
    to_core = remote(sq.at[0], sq_in.at[len(chips)], sq_send.at[len(chips)], sq_recv.at[len(chips)], c_id)
    to_core.start()
    to_core.wait()
    sq[1] = sq[0] + sq_in[len(chips)]
    to_chips = [remote(sq.at[1], sq_in.at[j], sq_send.at[j], sq_recv.at[j], chip_ids[j]) for j in range(len(chips))]
    for c in to_chips:
        c.start()
    for c in to_chips:
        c.wait()
    total = sq[1]
    for j in range(len(chips)):
        total = total + sq_in[j]
    norm_out[...] = total
    put_out.wait()
    put_ig.wait()


def layer_call(dims, x, dy, masks, wq, wp, wu, wd, vec):
    Z, Y, X = dims
    n = Z * Y * X * 2
    lay = Layout(n)
    T = x.shape[0]
    S = jax.ShapeDtypeStruct
    V = pltpu.VMEM
    dma = pltpu.SemaphoreType.DMA
    vm = pl.BlockSpec(memory_space=pltpu.VMEM)
    hbm = pl.BlockSpec(memory_space=pl.ANY)
    P1, P2, chips = Z - 1, X * Y - 1, Z * Y * X - 1
    peers = P1 + P2 + 1
    blocks = lay.blocks
    one_group = Z * Y * X * 2 <= 32
    scratch = [V((T, D), bf16), V((T, D), bf16), V(masks.shape, jnp.int32), V((T, D), bf16), V((T, 3 * D), bf16)]
    scratch += [V((T, D), f32), V((T, D), bf16), V((T, D), f32), V((T, D), f32), V((T, D), bf16)]
    scratch += [V((T, FF), bf16), V((T, FF), bf16)]
    scratch += [V((Z, Y, X, 2) + b, bf16) for b in blocks + ((16, 128),)]
    scratch += [V((D, 3 * D), bf16), V((D, D), bf16), V((D, FF), bf16), V((FF, D), bf16), V((16, D), f32), V((1, FF), f32)]
    scratch += [V((n, 128), f32), V((4, 16 * n, D) if one_group else (1, 16, 128), bf16)]
    scratch += [V((16, 128) if lay.straight else (FF, D), bf16), V((D, D), bf16)]
    scratch += [V(b, f32) for b in blocks + ((16, 128),)]
    scratch += [V((D, D), f32), V((8, D), f32), V((1, FF), f32)]
    scratch += [V((Z, Y, X) + b, bf16) for b in blocks]
    scratch += [V((P2, Z) + b, bf16) for b in blocks]
    scratch += [V((P1,) + b, bf16) for b in blocks]
    scratch += [V((3, 16, D), f32), V((P1, 16, D), f32), V((P2, 16, D), f32), V((1, 16, D), f32)]
    scratch += [V((2, 8, 128), f32), V((chips + 1, 8, 128), f32)]
    scratch += [dma((5,))] + [dma((6, peers))] * 4 + [dma((peers,))] * 2 + [dma((chips + 1,))] * 2
    return pl.pallas_call(
        functools.partial(layer_kernel, dims),
        out_shape=[
            S((T, D), bf16), S((T, D), f32), S((3,) + blocks[0], f32), S(blocks[3], f32), S(blocks[4], f32),
            S((16, D), f32), S((8, 128), f32),
        ],
        in_specs=[hbm] * 3 + [vm] * 5,
        out_specs=[hbm] * 2 + [vm] * 5,
        scratch_shapes=scratch,
        compiler_params=pltpu.CompilerParams(
            collective_id=0, has_side_effects=True, vmem_limit_bytes=62 * 1024 * 1024
        ),
        name="layer",
    )(x, dy, masks, wq, wp, wu, wd, vec)


def adam_step(w, m, r, g, rate, decay):
    m_new = BETA1 * m + (1.0 - BETA1) * g
    r_new = BETA2 * r + (1.0 - BETA2) * g * g
    m_hat = m_new / (1.0 - BETA1**STEP)
    r_hat = r_new / (1.0 - BETA2**STEP)
    return w - rate * (m_hat / (jnp.sqrt(r_hat) + ADAM_EPS) + decay * w), m_new, r_new


def adam_kernel(n, *refs):
    small, matrix_squares, gq, gu, gd = refs[0:5]
    state = refs[5:20]
    out_in, ig_in = refs[20:22]
    out_ref, ig_ref, norm = refs[22:25]
    new = refs[25:40]
    sem, out_v, ig_v = refs[40:43]
    lay = Layout(n)
    R, Rd, V = lay.R, lay.Rd, state[12].shape[1]
    T = out_v.shape[0]
    parts = [pl.ds(k * (T // 4), T // 4) for k in range(4)]
    loads = [pltpu.make_async_copy(out_in.at[r], out_v.at[r], sem.at[k]) for k, r in enumerate(parts)]
    loads += [pltpu.make_async_copy(ig_in.at[r], ig_v.at[r], sem.at[4 + k]) for k, r in enumerate(parts)]
    stores = [pltpu.make_async_copy(out_v.at[r], out_ref.at[r], sem.at[8 + k]) for k, r in enumerate(parts)]
    stores += [pltpu.make_async_copy(ig_v.at[r], ig_ref.at[r], sem.at[12 + k]) for k, r in enumerate(parts)]
    for c in loads:
        c.start()
    for c, d in zip(loads, stores):
        c.wait()
        d.start()
    vecs = small[0:10]
    squares = jnp.sum(jnp.sum(vecs * vecs, axis=0, keepdims=True), axis=1, keepdims=True) + matrix_squares[0:1, 0:1]
    clip = jnp.sqrt(squares)
    norm[...] = clip
    factor = 1.0 / clip

    def step(k, rows, cols, g, rate, decay):
        w, m, r = (ref[rows, cols] for ref in state[3 * k : 3 * k + 3])
        for ref, value in zip(new[3 * k : 3 * k + 3], adam_step(w, m, r, g * factor, rate, decay)):
            ref[rows, cols] = value

    every = slice(0, D)
    g = jnp.concatenate([gq[k, 0:R, 128 * j : 128 * j + 128] for j in range(3) for k in range(3)], axis=1)
    step(0, slice(0, R), slice(0, 3 * D), g, RATES[0], DECAY)
    for i in range(R):
        step(1, slice(i, i + 1), every, gq[i % 3, R + i // 3 : R + i // 3 + 1], RATES[1], DECAY)
    for cols, shift, at in lay.u:
        step(2, slice(0, R), cols, gu[shift : shift + R, at], RATES[2], DECAY)
    step(3, slice(0, Rd), every, gd[0:Rd], RATES[3], DECAY)
    me = lax.axis_index("dp") * (n // lax.axis_size("dp")) + lax.axis_index("fsdp")
    start = me * V
    row, lane = start // D, lax.rem(start, D)
    two = jnp.concatenate([small[pl.ds(row, 1), :], small[pl.ds(row + 1, 1), :]], axis=1)
    two = pltpu.roll(jnp.broadcast_to(two, (8, 2 * D)), 2 * D - lane, 1)
    step(4, slice(0, 1), slice(0, V), two[0:1, 0:V], VECTOR_RATE, 0.0)
    for c in stores:
        c.wait()


def adam_call(n, small, squares, gq, gu, gd, state, out, ig):
    vm = pl.BlockSpec(memory_space=pltpu.VMEM)
    hbm = pl.BlockSpec(memory_space=pl.ANY)
    S = jax.ShapeDtypeStruct
    return pl.pallas_call(
        functools.partial(adam_kernel, n),
        out_shape=[S(out.shape, out.dtype), S(ig.shape, ig.dtype), S((1, 1), f32)] + [S(s.shape, f32) for s in state],
        in_specs=[vm] * 20 + [hbm] * 2,
        out_specs=[hbm] * 2 + [vm] * 16,
        scratch_shapes=[pltpu.SemaphoreType.DMA((16,)), pltpu.VMEM(out.shape, out.dtype), pltpu.VMEM(ig.shape, ig.dtype)],
        name="adam",
    )(small, squares, gq, gu, gd, *state, out, ig)


def solution(mesh):
    n_dp, n_fs = mesh.shape["dp"], mesh.shape["fsdp"]
    X = n_fs // 2
    Y = X if n_dp % X == 0 else 1
    dims = (n_dp // Y, Y, X)
    n = n_dp * n_fs

    def per_device(x, dy, masks, *state):
        state = list(state)
        flat = [s.shape for s in state[12:15]]
        state[12:15] = [s.reshape(1, -1) for s in state[12:15]]
        out, ig, gq, gu, gd, small, squares = layer_call(
            dims, x, dy, masks, state[0], state[3], state[6], state[9], state[12]
        )
        res = adam_call(n, small, squares, gq, gu, gd, state, out, ig)
        new = list(res[3:])
        new[12:15] = [v.reshape(f) for v, f in zip(new[12:15], flat)]
        return (res[0], res[1], res[2].reshape(()), *new)

    rows = P(("dp", "fsdp"), None)
    line = P(("dp", "fsdp"))
    placed = (rows, rows, P(("dp", "fsdp"), None, None)) + (rows,) * 12 + (line,) * 3
    given = (rows, rows, P()) + (rows,) * 12 + (line,) * 3
    return jax.shard_map(per_device, mesh=mesh, in_specs=placed, out_specs=given, check_vma=False)
```

time: 191 us -> 110 us (0.58)
  Pallas kernels: 190 us -> 109 us
    pallas_call x1, Pallas kernels: 183 us -> 102 us  [layer_call(): pl.pallas_call(functools.partial(layer_kernel, dims), out_shape=[S((T, D)...]
where the time goes in v2:
time: 110 us; the launch traced here: 109 us
  Pallas kernels  109 us (99%)
    pallas_call x1, Pallas kernels, layer_call(): pl.pallas_call(functools.partial(layer_kernel, dims), out_shape=[S((T, D)...  102 us
    pallas_call x1, Pallas kernels, adam_call(): pl.pallas_call(functools.partial(adam_kernel, n), out_shape=[S(out.shape,...  6.7 us

profile of v2, /device:TPU:0, one launch (start us, length us, event | category | flops | bytes accessed | tf_op | source)
XLA Modules:
  0.0 109.5 jit_solution(15646189334670496523)
XLA Ops:
  0.7 101.9 %layer.1 = (bf16[2048,384]{1,0:T(8,128)(2,1)}, f32[2048,384]{1,0:T(8,128)}, f32[3,16,384]{2,1,0:T(8,128)}, f32[16,1536]{1,0:T(8,128)}, f32[48,384]{1,0:T(8,128)}, /*index=5*/f32[16,384]{1,0:T(8,128)}, f32[8,128]{1,0:T(8,128)}) custom-call(bf16[2048,384]{1,0:T(8,128)(2,1)} %refs_0_.1, bf16[2048,384]{1,0:T(8,128)(2,1)} %refs_1_.1, s32[32,64,64]{2,1,0:T(8,128)} %refs_2_.1, ...), custom_call_target="tpu_custom_call" | custom-call | tf_op jit(solution)/shard_map/layer/pallas_call | solution.py:580
  102.6 6.7 %adam.1 = (bf16[2048,384]{1,0:T(8,128)(2,1)}, f32[2048,384]{1,0:T(8,128)}, f32[1,1]{1,0:T(1,128)}, f32[12,1152]{1,0:T(8,128)}, f32[12,1152]{1,0:T(8,128)}, /*ind...) custom-call(f32[16,384]{1,0:T(8,128)} %get-tuple-element.43.refs_0_,, ...), custom_call_target="tpu_custom_call" | custom-call | tf_op jit(solution)/shard_map/adam/pallas_call | solution.py:657

commit v3 on v2

v3 whole, which is shorter than its diff:
```python
import functools
import math

import jax
import jax.numpy as jnp
from jax import lax
from jax.experimental import pallas as pl
from jax.experimental.pallas import tpu as pltpu
from jax.sharding import PartitionSpec as P

D = 384
FF = 1536
HD = 64
STEP = 10
NORM_EPS = 1e-05
BETA1 = 0.9
BETA2 = 0.999
ADAM_EPS = 1e-08
DECAY = 0.05
RATES = (0.1, 0.5, 0.1, 0.05)
VECTOR_RATE = 1.0
TB = 512
TA = 1024
TM = 1024
CH = 256

f32 = jnp.float32
bf16 = jnp.bfloat16
NN = (((1,), (0,)), ((), ()))
NT = (((1,), (1,)), ((), ()))
TN = (((0,), (0,)), ((), ()))
MESH = pl.DeviceIdType.MESH


def dot(a, b, dims=NN):
    return lax.dot_general(a, b, dims, preferred_element_type=f32)


def ln_parts(v):
    centered = v - jnp.mean(v, axis=-1, keepdims=True)
    variance = jnp.mean(centered * centered, axis=-1, keepdims=True)
    return centered, lax.rsqrt(variance + NORM_EPS)


def ln_back(grad, xhat, rstd, gain):
    t = grad * gain
    m1 = jnp.mean(t, axis=-1, keepdims=True)
    m2 = jnp.mean(t * xhat, axis=-1, keepdims=True)
    return rstd * (t - m1 - xhat * m2)


def gelu_parts(u):
    cdf = 0.5 + 0.5 * lax.erf(u * (2.0**-0.5))
    density = jnp.exp2(u * u * (-0.5 * math.log2(math.e))) * (1.0 / math.sqrt(2 * math.pi))
    return u * cdf, cdf + u * density


def lane_left():
    return lax.broadcasted_iota(jnp.int32, (64, 128), 1) < 64


def two_heads(m, left):
    zero = jnp.zeros_like(m)
    return jnp.concatenate([jnp.where(left, m, zero), jnp.where(left, zero, m)], axis=0)


def diagonal(r, left):
    return jnp.where(left, r[0:64], r[64:128])


def attention_forward(i, g, mask, qkv, probs, mixed):
    left = lane_left()
    across = slice(128 * g, 128 * g + 128)
    clouds = TA // 64
    rows = [pl.ds(pl.multiple_of(i * TA + 64 * c, 64), 64) for c in range(clouds)]
    held = []
    for c, r in enumerate(rows):
        b = jnp.where(mask[i * clouds + c] == 1, 0.0, -1e30)
        q = qkv[r, D * g : D * g + 128] * jnp.asarray(0.125, bf16)
        k = qkv[r, D * g + 128 : D * g + 256]
        held.append(dot(k, two_heads(q, left), NT) + jnp.concatenate([b, b], axis=1))
    for c, r in enumerate(rows):
        s = held[c]
        e = jnp.exp(s - jnp.max(s, axis=0, keepdims=True))
        p = e * (1.0 / jnp.sum(e, axis=0, keepdims=True))
        probs[r, across] = p
        held[c] = p.astype(bf16)
    for c, r in enumerate(rows):
        v = qkv[r, D * g + 256 : D * g + 384]
        mixed[r, across] = diagonal(dot(held[c], v, TN), left).astype(bf16)


def attention_backward(i, g, qkv, probs, dmix, dqkv):
    left = lane_left()
    across = slice(128 * g, 128 * g + 128)
    rows = [pl.ds(pl.multiple_of(i * TA + 64 * c, 64), 64) for c in range(TA // 64)]
    held = []
    for r in rows:
        v = qkv[r, D * g + 256 : D * g + 384]
        held.append(dot(v, two_heads(dmix[r, across], left), NT))
    for c, r in enumerate(rows):
        p, dp = probs[r, across], held[c]
        held[c] = (p * (dp - jnp.sum(p * dp, axis=0, keepdims=True))).astype(bf16)
    for ds, r in zip(held, rows):
        q = qkv[r, D * g : D * g + 128] * jnp.asarray(0.125, bf16)
        k = qkv[r, D * g + 128 : D * g + 256]
        dv = dot(probs[r, across].astype(bf16), two_heads(dmix[r, across], left))
        dk = dot(ds, two_heads(q, left))
        dq = diagonal(dot(ds, k, TN), left) * 0.125
        dqkv[r, D * g : D * g + 128] = dq.astype(bf16)
        dqkv[r, D * g + 128 : D * g + 256] = dk.astype(bf16)
        dqkv[r, D * g + 256 : D * g + 384] = dv.astype(bf16)


def pick_rows(devs, total, shift, step, k, block=None):
    rows = total // devs[2]
    shape = (16 * devs[1], total if block is None else D)
    out = lax.broadcasted_iota(jnp.int32, shape, 0)
    col = lax.broadcasted_iota(jnp.int32, shape, 1)
    if block is not None:
        col = col + D * block
    dev = out >> 4
    i = out - 16 * dev - shift
    ok = (i >= 0) & (i < rows // step) & (col == rows * (dev + devs[0]) + step * i + k)
    return jnp.where(ok, 1.0, 0.0).astype(bf16)


class Layout:
    def __init__(self, n):
        self.n, self.R, self.Rd = n, D // n, FF // n
        self.straight = self.Rd % 16 == 0
        self.cuts = self.Rd // 16 if self.straight else 1
        self.cw = FF // self.cuts
        self.up = self.cw if self.straight else D
        if self.straight:
            self.pieces = [
                (self.Rd * d + 16 * k, self.cw * k + 16 * d, k, 16 * d) for k in range(self.cuts) for d in range(n)
            ]
        self.blocks = ((16, D),) * 3 + ((16, self.up + D),) * self.cuts
        self.chunks = len(self.blocks)


def layer_kernel(dims, *refs):
    Z, Y, X = dims
    n = Z * Y * X * 2
    lay = Layout(n)
    R, Rd, NC, VEC = lay.R, lay.Rd, lay.chunks, lay.chunks
    MLP = list(range(3, NC))
    it = iter(refs)

    def take(count=None):
        return next(it) if count is None else [next(it) for _ in range(count)]

    x_hbm, dy_hbm, mask_hbm, wq_own, wp_own, wu_own, wd_own, vec_own = take(8)
    out_hbm, ig_hbm, gq_out, gm_out, small_out, norm_out = take(6)
    x, dy, mask, a, qkv, probs, mixed, h1, dh1, c_all, z_all, du_all = take(12)
    bufs = take(NC + 1)
    wq, wp, wu, wd, vec, bu, vgrid, sel, tmp_q = take(9)
    stage = take(NC + 1)
    acc_p, dvec, dbu = take(3)
    r1, r2, r3 = take(NC), take(NC), take(NC)
    small, s1, s2, s3, sq, sq_in = take(6)
    local_sem, ag_send, ag_recv, rs_send, rs_recv, ar_send, ar_recv, sq_send, sq_recv = take(9)
    outs = [gq_out.at[k] for k in range(3)] + [gm_out.at[k] for k in range(lay.cuts)]

    T = x.shape[0]
    V = vec_own.shape[1]
    dp = lax.axis_index("dp")
    fs = lax.axis_index("fsdp")
    z, y = dp // Y, lax.rem(dp, Y)
    xx, core = fs // 2, lax.rem(fs, 2)

    loads = [
        pltpu.make_async_copy(x_hbm, x, local_sem.at[0]),
        pltpu.make_async_copy(mask_hbm, mask, local_sem.at[1]),
        pltpu.make_async_copy(dy_hbm, dy, local_sem.at[2]),
    ]
    for c in loads:
        c.start()

    chips = [
        (lax.rem(z + k // (X * Y), Z), lax.rem(y + k // X % Y, Y), lax.rem(xx + k % X, X)) for k in range(1, Z * Y * X)
    ]
    chip_ids = [(c[0] * Y + c[1], c[2] * 2 + core) for c in chips]
    in_z = [k * X * Y - 1 for k in range(1, Z)]
    in_p = list(range(X * Y - 1))
    z_peers, z_ids = [chips[k] for k in in_z], [chip_ids[k] for k in in_z]
    p_peers, p_ids = [chips[k] for k in in_p], [chip_ids[k] for k in in_p]
    c_id = (dp, fs + 1 - 2 * core)
    P1, P2 = len(z_ids), len(p_ids)

    barrier = pltpu.get_barrier_semaphore()
    for dev in chip_ids + [c_id]:
        pl.semaphore_signal(barrier, inc=1, device_id=dev, device_id_type=MESH)

    for t in stage:
        t[...] = jnp.zeros_like(t)
    for g in range(3):
        for j in range(3):
            stage[g][0:R, 128 * j : 128 * j + 128] = wq_own[:, D * j + 128 * g : D * j + 128 * g + 128]
    for i in range(R):
        stage[i % 3][R + i // 3 : R + i // 3 + 1] = wp_own[i : i + 1]
    stage[VEC][0:1, 0:V] = vec_own[...]
    for ch in (0, 1, 2, VEC):
        bufs[ch][z, y, xx, core] = stage[ch][...].astype(bf16)

    pl.semaphore_wait(barrier, len(chip_ids) + 1)

    def remote(src, dst, send, recv, dev):
        return pltpu.make_async_remote_copy(
            src_ref=src, dst_ref=dst, send_sem=send, recv_sem=recv, device_id=dev, device_id_type=MESH
        )

    def gather(ch, stage):
        g = bufs[ch]
        send, recv = ag_send.at[ch], ag_recv.at[ch]
        if stage == 0:
            own = g.at[z, y, xx, core]
            return [remote(own, own, send.at[j], recv.at[j], z_ids[j]) for j in range(P1)]
        if stage == 1:
            own = g.at[:, y, xx, core]
            return [remote(own, own, send.at[P1 + j], recv.at[P1 + j], p_ids[j]) for j in range(P2)]
        own = g.at[:, :, :, core]
        return [remote(own, own, send.at[P1 + P2], recv.at[P1 + P2], c_id)]

    def gather_step(ch, stage):
        if stage > 0:
            for c in gather(ch, stage - 1):
                c.wait()
        if stage < 3:
            for c in gather(ch, stage):
                c.start()

    def scatter(ch, stage):
        g = bufs[ch]
        send, recv = rs_send.at[ch], rs_recv.at[ch]
        if stage == 0:
            return [remote(g.at[:, :, :, 1 - core], r1[ch], send.at[P1 + P2], recv.at[P1 + P2], c_id)]
        if stage == 1:
            return [
                remote(g.at[:, p_peers[j][1], p_peers[j][2], core], r2[ch].at[j], send.at[P1 + j], recv.at[P1 + j], p_ids[j])
                for j in range(P2)
            ]
        return [
            remote(g.at[z_peers[j][0], y, xx, core], r3[ch].at[j], send.at[j], recv.at[j], z_ids[j]) for j in range(P1)
        ]

    def scatter_step(ch, stage):
        g = bufs[ch]
        if stage > 0:
            for c in scatter(ch, stage - 1):
                c.wait()
        if stage == 1:
            @pl.loop(0, Z)
            def _(zz):
                for yy in range(Y):
                    for cx in range(X):
                        t = g[zz, yy, cx, core].astype(f32) + r1[ch][zz, yy, cx].astype(f32)
                        g[zz, yy, cx, core] = t.astype(bf16)
        elif stage == 2:
            for zz in range(Z):
                t = g[zz, y, xx, core].astype(f32)
                for j in range(P2):
                    t = t + r2[ch][j, zz].astype(f32)
                g[zz, y, xx, core] = t.astype(bf16)
        elif stage == 3:
            t = g[z, y, xx, core].astype(f32)
            for j in range(P1):
                t = t + r3[ch][j].astype(f32)
            outs[ch][...] = t
        if stage < 3:
            for c in scatter(ch, stage):
                c.start()

    per_z = 2 * X * Y
    z_group = max(1, min(Z, 32 // per_z))
    count = z_group * per_z
    n_groups = Z // z_group
    SEL = {(0, 1, 0): 0, (R, 3, 0): 1, (R, 3, 1): 2, (R, 3, 2): 3}

    def pick(k, rows, shift, step, first, block=None):
        if n_groups == 1 and (shift, step, first) in SEL and rows == D:
            return sel[SEL[shift, step, first]]
        return pick_rows((k * count, count, n), rows, shift, step, first, block)

    def by_groups(f):
        if n_groups == 1:
            f(0)
        else:
            pl.loop(0, n_groups)(f)

    def unpack(into, cols, terms):
        def part(k):
            total = None
            for g, at, rows, shift, step, first, block in terms:
                flat = g[pl.ds(k * z_group, z_group), :, :, :, :, at].reshape(16 * count, at.stop - at.start)
                t = dot(pick(k, rows, shift, step, first, block), flat, TN)
                total = t if total is None else total + t
            if n_groups == 1:
                into[:, cols] = total.astype(bf16)
            else:
                into[:, cols] = (into[:, cols].astype(f32) + total).astype(bf16)

        if n_groups > 1:
            into[:, cols] = jnp.zeros((into.shape[0], cols.stop - cols.start), bf16)
        by_groups(part)

    def pack(g, at, terms, more=False):
        def one(k):
            total = None
            for source, rows, shift, step, first, block in terms:
                t = dot(pick(k, rows, shift, step, first, block), source[...])
                total = t if total is None else total + t
            where = pl.ds(k * z_group, z_group)
            total = total.reshape((z_group,) + g.shape[1:5] + (total.shape[1],))
            if more:
                total = total + g[where, :, :, :, :, at].astype(f32)
            g[where, :, :, :, :, at] = total.astype(bf16)

        by_groups(one)

    every = slice(0, D)

    for ch in (VEC, 0, 1, 2):
        gather_step(ch, 0)
    if lay.straight:
        for nat, _, k, at in lay.pieces:
            stage[3 + k][0:R, at : at + 16] = wu_own[:, nat : nat + 16]
        for k in range(lay.cuts):
            stage[3 + k][:, lay.up : lay.up + D] = wd_own[16 * k : 16 * k + 16]
    else:
        for k in range(FF // D):
            stage[3][R * k : R * k + R, 0:D] = wu_own[:, D * k : D * k + D]
        stage[3][0:Rd, D : 2 * D] = wd_own[...]
    for ch in MLP:
        bufs[ch][z, y, xx, core] = stage[ch][...].astype(bf16)
        gather_step(ch, 0)
    if n_groups == 1:
        for (shift, step, first), k in SEL.items():
            sel[k] = pick_rows((0, n, n), D, shift, step, first)
    for r in (acc_p, dvec, dbu):
        r[...] = jnp.zeros_like(r)
    for c in loads:
        c.wait()

    @pl.loop(0, T // TB)
    def _(i):
        rows = pl.ds(pl.multiple_of(i * TB, TB), TB)
        centered, rstd = ln_parts(x[rows, :].astype(f32))
        h1[rows, :] = centered * rstd
        key = lax.broadcasted_iota(jnp.int32, (64, 64), 0)
        query = lax.broadcasted_iota(jnp.int32, (64, 64), 1)
        clouds = TB // 64
        for c in range(clouds):
            allowed = (key <= query) & ((mask[i * clouds + c].T == 1) | (key == query))
            mask[i * clouds + c] = jnp.where(allowed, 1, 0)

    for ch in (VEC, 0, 1, 2):
        gather_step(ch, 1)
    gather_step(MLP[0], 1)
    dvec[5:6] = jnp.sum(dy[...].astype(f32), axis=0, keepdims=True)
    gather_step(VEC, 2)
    gather_step(0, 2)
    gather_step(VEC, 3)
    for k in range(n_groups):
        row = lax.broadcasted_iota(jnp.int32, (count, 16 * count), 0)
        col = lax.broadcasted_iota(jnp.int32, (count, 16 * count), 1)
        pick_vec = jnp.where(col == 16 * row, 1.0, 0.0).astype(bf16)
        flat = bufs[VEC][k * z_group : (k + 1) * z_group].reshape(16 * count, 128)
        vgrid[k * count : (k + 1) * count] = dot(pick_vec, flat)
    for d in range(n):
        start, stop = V * d, V * d + V
        while start < stop:
            r0, l0 = start // D, start % D
            size = min(stop - start, D - l0)
            o = start - V * d
            vec[r0 : r0 + 1, l0 : l0 + size] = vgrid[d : d + 1, o : o + size]
            start += size

    def pair_forward(g):
        gather_step(g, 3)
        mine = slice(D * g, D * g + D)
        unpack(wq, mine, [(bufs[g], every, D, 0, 1, 0, None)])

        @pl.loop(0, T // TA)
        def _(i):
            @pl.when(i == 1)
            def _():
                if g < 2:
                    gather_step(g + 1, 2)
                    if len(MLP) > g + 1:
                        gather_step(MLP[g + 1], 1)
                else:
                    gather_step(MLP[0], 2)

            rows = pl.ds(pl.multiple_of(i * TA, TA), TA)
            if g == 0:
                av = (h1[rows, :] * vec[0:1] + vec[1:2]).astype(bf16)
                a[rows, :] = av
            else:
                av = a[rows, :]
            qkv[rows, mine] = dot(av, wq[:, mine]).astype(bf16)
            attention_forward(i, g, mask, qkv, probs, mixed)

    for g in range(3):
        pair_forward(g)
    unpack(wp, every, [(bufs[k], every, D, R, 3, k, None) for k in range(3)])
    if lay.straight:
        for nat, place, _, _ in lay.pieces:
            r0, l0 = 6 + nat // D, nat % D
            bu[:, place : place + 16] = vec[r0 : r0 + 1, l0 : l0 + 16]
    else:
        for k in range(FF // D):
            bu[:, D * k : D * k + D] = vec[6 + k : 7 + k]

    @pl.loop(0, T // TB)
    def _(i):
        @pl.when(i == 2)
        def _():
            if len(MLP) > 1:
                gather_step(MLP[1], 2)

        rows = pl.ds(pl.multiple_of(i * TB, TB), TB)
        h = x[rows, :].astype(f32) + (dot(mixed[rows, :], wp[...]) + vec[4:5])
        h1[rows, :] = h
        centered, rstd = ln_parts(h)
        c_all[rows, :] = (centered * rstd * vec[2:3] + vec[3:4]).astype(bf16)

    for k in range(lay.cuts):
        ch = 3 + k
        cut = slice(lay.cw * k, lay.cw * k + lay.cw)
        gather_step(ch, 3)
        if lay.straight:
            unpack(wu, cut, [(bufs[ch], slice(0, lay.up), D, 0, 1, 0, None)])
            wd[cut, :] = bufs[ch][:, :, :, :, :, lay.up : lay.up + D].reshape(lay.cw, D)
        else:
            for j in range(FF // D):
                unpack(wu, slice(D * j, D * j + D), [(bufs[ch], every, D, R * j, 1, 0, None)])
                unpack(wd.at[D * j : D * j + D], every, [(bufs[ch], slice(D, 2 * D), FF, 0, 1, 0, j)])

        @pl.loop(0, T // TM)
        def _(i):
            @pl.when(i == 1)
            def _():
                if k == 0 and lay.cuts > 2:
                    gather_step(MLP[2], 2)
                if k > 0:
                    scatter_step(ch - 1, 1)

            rows = pl.ds(pl.multiple_of(i * TM, TM), TM)
            c, dyv = c_all[rows, :], dy[rows, :]
            for start in range(cut.start, cut.stop, CH):
                ns = slice(start, start + CH)
                u = dot(c, wu[:, ns]) + bu[:, ns]
                dz = dot(dyv, wd[ns, :], NT)
                zv, slope = gelu_parts(u)
                z_all[rows, ns] = zv.astype(bf16)
                du = (dz * slope).astype(bf16)
                du_all[rows, ns] = du
                dbu[:, ns] += jnp.sum(du.astype(f32), axis=0, keepdims=True)

        if lay.straight:
            g = bufs[ch]
            down = dot(dy[...], z_all[:, cut], TN).astype(bf16).T
            g[:, :, :, :, :, lay.up : lay.up + D] = down.reshape(g.shape[:5] + (D,))
            pack(g, slice(0, lay.up), [(dot(c_all[...], du_all[:, cut], TN).astype(bf16), D, 0, 1, 0, None)])
        else:
            for j in range(FF // D):
                cols = slice(D * j, D * j + D)
                tmp_q[...] = dot(dy[...], z_all[:, cols], TN).astype(bf16).T
                pack(bufs[ch], slice(D, 2 * D), [(tmp_q, FF, 0, 1, 0, j)], j > 0)
                tmp_q[...] = dot(c_all[...], du_all[:, cols], TN).astype(bf16)
                pack(bufs[ch], every, [(tmp_q, D, R * j, 1, 0, None)], j > 0)
        scatter_step(ch, 0)

    dmix = mixed

    @pl.loop(0, T // TM)
    def _(i):
        @pl.when(i == 1)
        def _():
            scatter_step(MLP[-1], 1)
            if len(MLP) > 1:
                scatter_step(MLP[0], 2)

        rows = pl.ds(pl.multiple_of(i * TM, TM), TM)
        dc = dot(du_all[rows, :], wu[...], NT)
        centered, rstd = ln_parts(h1[rows, :])
        xhat = centered * rstd
        dvec[2:3] += jnp.sum(dc * xhat, axis=0, keepdims=True)
        dvec[3:4] += jnp.sum(dc, axis=0, keepdims=True)
        d1 = dy[rows, :].astype(f32) + ln_back(dc, xhat, rstd, vec[2:3])
        dh1[rows, :] = d1
        dr = d1.astype(bf16)
        dvec[4:5] += jnp.sum(dr.astype(f32), axis=0, keepdims=True)
        acc_p[...] += dot(mixed[rows, :], dr, TN)
        dmix[rows, :] = dot(dr, wp[...], NT).astype(bf16)

    wp[...] = acc_p[...].astype(bf16)

    small[0] = jnp.zeros((16, D), f32)
    small[0, 2:6] = dvec[2:6]
    if lay.straight:
        for nat, place, _, _ in lay.pieces:
            r0, l0 = 6 + nat // D, nat % D
            small[0, r0 : r0 + 1, l0 : l0 + 16] = dbu[:, place : place + 16]
    else:
        for k in range(FF // D):
            small[0, 6 + k : 7 + k] = dbu[:, D * k : D * k + D]
    received = (s1, s2, s3)

    def spread(stage):
        if stage == 0:
            return [remote(small.at[0], s1.at[j], ar_send.at[j], ar_recv.at[j], z_ids[j]) for j in range(P1)]
        if stage == 1:
            return [remote(small.at[1], s2.at[j], ar_send.at[P1 + j], ar_recv.at[P1 + j], p_ids[j]) for j in range(P2)]
        return [remote(small.at[2], s3.at[0], ar_send.at[P1 + P2], ar_recv.at[P1 + P2], c_id)]

    def spread_step(stage):
        if stage > 0:
            copies = spread(stage - 1)
            for c in copies:
                c.wait()
            t = small[stage - 1]
            for j in range(len(copies)):
                t = t + received[stage - 1][j]
            if stage < 3:
                small[stage] = t
            else:
                small_out[...] = t
        if stage < 3:
            for c in spread(stage):
                c.start()

    spread_step(0)

    dqkv = du_all

    def pair_backward(g):
        @pl.loop(0, T // TA)
        def _(i):
            attention_backward(i, g, qkv, probs, dmix, dqkv)

        if g == 0 and len(MLP) > 2:
            scatter_step(MLP[1], 2)
        if g == 2:
            spread_step(1)
        if g > 0:
            scatter_step(g - 1, 1)
        if g == 1 and len(MLP) > 1:
            scatter_step(MLP[0], 3)
        if g == 2:
            scatter_step(MLP[-1], 2)
        tmp_q[...] = dot(a[...], dqkv[:, D * g : D * g + D], TN).astype(bf16)
        pack(bufs[g], every, [(tmp_q, D, 0, 1, 0, None), (wp, D, R, 3, g, None)])
        scatter_step(g, 0)

    for g in range(3):
        pair_backward(g)

    @pl.loop(0, T // TB)
    def _(i):
        @pl.when(i == 1)
        def _():
            scatter_step(2, 1)
            scatter_step(0, 2)

        @pl.when(i == 3)
        def _():
            if len(MLP) > 2:
                scatter_step(MLP[1], 3)
            scatter_step(1, 2)
            spread_step(2)

        rows = pl.ds(pl.multiple_of(i * TB, TB), TB)
        da = dot(dqkv[rows, 0 : 3 * D], wq[...], NT)
        centered, rstd = ln_parts(x[rows, :].astype(f32))
        xhat = centered * rstd
        dvec[0:1] += jnp.sum(da * xhat, axis=0, keepdims=True)
        dvec[1:2] += jnp.sum(da, axis=0, keepdims=True)
        dh1[rows, :] = dh1[rows, :] + ln_back(da, xhat, rstd, vec[0:1])

    put_ig = pltpu.make_async_copy(dh1, ig_hbm, local_sem.at[4])
    put_ig.start()

    @pl.loop(0, T // TB)
    def _(i):
        @pl.when(i == 1)
        def _():
            scatter_step(MLP[-1], 3)
            scatter_step(0, 3)

        @pl.when(i == 2)
        def _():
            scatter_step(2, 2)

        rows = pl.ds(pl.multiple_of(i * TB, TB), TB)
        dy[rows, :] = (h1[rows, :] + (dot(z_all[rows, :], wd[...]) + vec[5:6])).astype(bf16)

    put_out = pltpu.make_async_copy(dy, out_hbm, local_sem.at[3])
    put_out.start()

    squares = jnp.zeros((1, 1), f32)
    spread_step(3)
    for ch in MLP + [0, 1, 2]:
        if ch in (1, 2):
            scatter_step(ch, 3)
        t = outs[ch][...]
        squares = squares + jnp.sum(jnp.sum(t * t, axis=0, keepdims=True), axis=1, keepdims=True)
    for j in range(6):
        sq[0, j : j + 1] = dvec[j // 3 : j // 3 + 1, 128 * (j % 3) : 128 * (j % 3) + 128]
    sq[0, 6:8] = jnp.broadcast_to(squares, (2, 128))
    to_core = remote(sq.at[0], sq_in.at[len(chips)], sq_send.at[len(chips)], sq_recv.at[len(chips)], c_id)
    to_core.start()
    to_core.wait()
    sq[1] = sq[0] + sq_in[len(chips)]
    to_chips = [remote(sq.at[1], sq_in.at[j], sq_send.at[j], sq_recv.at[j], chip_ids[j]) for j in range(len(chips))]
    for c in to_chips:
        c.start()
    for c in to_chips:
        c.wait()
    total = sq[1]
    for j in range(len(chips)):
        total = total + sq_in[j]
    norm_out[...] = total
    for j in range(6):
        small_out[j // 3 : j // 3 + 1, 128 * (j % 3) : 128 * (j % 3) + 128] = total[j : j + 1]
    put_out.wait()
    put_ig.wait()


def layer_call(dims, x, dy, masks, wq, wp, wu, wd, vec):
    Z, Y, X = dims
    n = Z * Y * X * 2
    lay = Layout(n)
    T = x.shape[0]
    S = jax.ShapeDtypeStruct
    V = pltpu.VMEM
    dma = pltpu.SemaphoreType.DMA
    vm = pl.BlockSpec(memory_space=pltpu.VMEM)
    hbm = pl.BlockSpec(memory_space=pl.ANY)
    P1, P2, chips = Z - 1, X * Y - 1, Z * Y * X - 1
    peers = P1 + P2 + 1
    blocks, NC = lay.blocks, lay.chunks
    one_group = n <= 32
    scratch = [V((T, D), bf16), V((T, D), bf16), V(masks.shape, jnp.int32), V((T, D), bf16), V((T, 3 * D), bf16)]
    scratch += [V((T, D), f32), V((T, D), bf16), V((T, D), f32), V((T, D), f32), V((T, D), bf16)]
    scratch += [V((T, FF), bf16), V((T, FF), bf16)]
    scratch += [V((Z, Y, X, 2) + b, bf16) for b in blocks + ((16, 128),)]
    scratch += [V((D, 3 * D), bf16), V((D, D), bf16), V((D, FF), bf16), V((FF, D), bf16), V((16, D), f32), V((1, FF), f32)]
    scratch += [V((n, 128), f32), V((4, 16 * n, D) if one_group else (1, 16, 128), bf16), V((D, D), bf16)]
    scratch += [V(b, f32) for b in blocks + ((16, 128),)]
    scratch += [V((D, D), f32), V((8, D), f32), V((1, FF), f32)]
    scratch += [V((Z, Y, X) + b, bf16) for b in blocks]
    scratch += [V((P2, Z) + b, bf16) for b in blocks]
    scratch += [V((P1,) + b, bf16) for b in blocks]
    scratch += [V((3, 16, D), f32), V((P1, 16, D), f32), V((P2, 16, D), f32), V((1, 16, D), f32)]
    scratch += [V((2, 8, 128), f32), V((chips + 1, 8, 128), f32)]
    scratch += [dma((5,))] + [dma((NC + 1, peers))] * 4 + [dma((peers,))] * 2 + [dma((chips + 1,))] * 2
    return pl.pallas_call(
        functools.partial(layer_kernel, dims),
        out_shape=[
            S((T, D), bf16), S((T, D), f32), S((3,) + blocks[0], f32), S((lay.cuts,) + blocks[3], f32),
            S((16, D), f32), S((8, 128), f32),
        ],
        in_specs=[hbm] * 3 + [vm] * 5,
        out_specs=[hbm] * 2 + [vm] * 4,
        scratch_shapes=scratch,
        compiler_params=pltpu.CompilerParams(
            collective_id=0, has_side_effects=True, vmem_limit_bytes=62 * 1024 * 1024
        ),
        name="layer",
    )(x, dy, masks, wq, wp, wu, wd, vec)


def adam_step(w, m, r, g, rate, decay):
    m_new = BETA1 * m + (1.0 - BETA1) * g
    r_new = BETA2 * r + (1.0 - BETA2) * g * g
    m_hat = m_new / (1.0 - BETA1**STEP)
    r_hat = r_new / (1.0 - BETA2**STEP)
    return w - rate * (m_hat / (jnp.sqrt(r_hat) + ADAM_EPS) + decay * w), m_new, r_new


def adam_kernel(n, *refs):
    small, matrix_squares, gq, gm = refs[0:4]
    state = refs[4:19]
    out_in, ig_in = refs[19:21]
    out_ref, ig_ref, norm = refs[21:24]
    new_hbm = refs[24:39]
    sem, out_v, ig_v, up = refs[39:43]
    new = refs[43:58]
    lay = Layout(n)
    R, Rd, V = lay.R, lay.Rd, state[12].shape[1]
    T = out_v.shape[0]
    pieces = 4
    parts = [pl.ds(k * (T // pieces), T // pieces) for k in range(pieces)]
    moves = [(a, b, c, r) for r in parts for a, b, c in ((ig_in, ig_v, ig_ref), (out_in, out_v, out_ref))]
    loads = [pltpu.make_async_copy(a.at[r], b.at[r], sem.at[k]) for k, (a, b, c, r) in enumerate(moves)]
    stores = [pltpu.make_async_copy(b.at[r], c.at[r], sem.at[k + len(moves)]) for k, (a, b, c, r) in enumerate(moves)]
    for c in loads:
        c.start()
    puts = [pltpu.make_async_copy(a, b, sem.at[2 * len(moves) + k]) for k, (a, b) in enumerate(zip(new, new_hbm))]
    vecs = small[0:10]
    squares = jnp.sum(jnp.sum(vecs * vecs, axis=0, keepdims=True), axis=1, keepdims=True) + matrix_squares[6:7, 0:1]
    clip = jnp.sqrt(squares)
    norm[...] = clip
    factor = 1.0 / clip

    def step(k, rows, cols, g, rate, decay):
        w, m, r = (ref[rows, cols] for ref in state[3 * k : 3 * k + 3])
        for ref, value in zip(new[3 * k : 3 * k + 3], adam_step(w, m, r, g * factor, rate, decay)):
            ref[rows, cols] = value

    def put(k):
        for c in puts[3 * k : 3 * k + 3]:
            c.start()

    for c, d in zip(loads, stores):
        c.wait()
        d.start()
    every = slice(0, D)
    if lay.straight:
        for nat, _, k, at in lay.pieces:
            up[:, nat : nat + 16] = gm[k, 0:R, at : at + 16]
        down = jnp.concatenate([gm[k, :, lay.up : lay.up + D] for k in range(lay.cuts)], axis=0)
    else:
        for k in range(FF // D):
            up[:, D * k : D * k + D] = gm[0, R * k : R * k + R, 0:D]
        down = gm[0, 0:Rd, D : 2 * D]
    step(2, slice(0, R), slice(0, FF), up[...], RATES[2], DECAY)
    put(2)
    step(3, slice(0, Rd), every, down, RATES[3], DECAY)
    put(3)
    g = jnp.concatenate([gq[k, 0:R, 128 * j : 128 * j + 128] for j in range(3) for k in range(3)], axis=1)
    step(0, slice(0, R), slice(0, 3 * D), g, RATES[0], DECAY)
    put(0)
    g = jnp.concatenate([gq[i % 3, R + i // 3 : R + i // 3 + 1] for i in range(R)], axis=0)
    step(1, slice(0, R), every, g, RATES[1], DECAY)
    put(1)
    me = lax.axis_index("dp") * (n // lax.axis_size("dp")) + lax.axis_index("fsdp")
    start = me * V
    row, lane = start // D, lax.rem(start, D)
    two = jnp.concatenate([small[pl.ds(row, 1), :], small[pl.ds(row + 1, 1), :]], axis=1)
    two = pltpu.roll(jnp.broadcast_to(two, (8, 2 * D)), 2 * D - lane, 1)
    step(4, slice(0, 1), slice(0, V), two[0:1, 0:V], VECTOR_RATE, 0.0)
    put(4)
    for c in stores + puts:
        c.wait()


def adam_call(n, small, squares, gq, gm, state, out, ig):
    vm = pl.BlockSpec(memory_space=pltpu.VMEM)
    hbm = pl.BlockSpec(memory_space=pl.ANY)
    S = jax.ShapeDtypeStruct
    V = pltpu.VMEM
    return pl.pallas_call(
        functools.partial(adam_kernel, n),
        out_shape=[S(out.shape, out.dtype), S(ig.shape, ig.dtype), S((1, 1), f32)] + [S(s.shape, f32) for s in state],
        in_specs=[vm] * 19 + [hbm] * 2,
        out_specs=[hbm] * 2 + [vm] + [hbm] * 15,
        scratch_shapes=[pltpu.SemaphoreType.DMA((31,)), V(out.shape, out.dtype), V(ig.shape, ig.dtype)]
        + [V((D // n, FF), f32)]
        + [V(s.shape, f32) for s in state],
        name="adam",
    )(small, squares, gq, gm, *state, out, ig)


def solution(mesh):
    n_dp, n_fs = mesh.shape["dp"], mesh.shape["fsdp"]
    X = n_fs // 2
    Y = X if n_dp % X == 0 else 1
    dims = (n_dp // Y, Y, X)
    n = n_dp * n_fs

    def per_device(x, dy, masks, *state):
        state = list(state)
        flat = [s.shape for s in state[12:15]]
        state[12:15] = [s.reshape(1, -1) for s in state[12:15]]
        out, ig, gq, gm, small, squares = layer_call(
            dims, x, dy, masks, state[0], state[3], state[6], state[9], state[12]
        )
        res = adam_call(n, small, squares, gq, gm, state, out, ig)
        new = list(res[3:])
        new[12:15] = [v.reshape(f) for v, f in zip(new[12:15], flat)]
        return (res[0], res[1], res[2].reshape(()), *new)

    rows = P(("dp", "fsdp"), None)
    line = P(("dp", "fsdp"))
    placed = (rows, rows, P(("dp", "fsdp"), None, None)) + (rows,) * 12 + (line,) * 3
    given = (rows, rows, P()) + (rows,) * 12 + (line,) * 3
    return jax.shard_map(per_device, mesh=mesh, in_specs=placed, out_specs=given, check_vma=False)
```

time: 110 us -> 97.2 us (0.88)
  Pallas kernels: 109 us -> 96.2 us
    pallas_call x1, Pallas kernels: 102 us -> 89.8 us  [layer_call(): pl.pallas_call(functools.partial(layer_kernel, dims), out_shape=[S((T, D)...]
where the time goes in v3:
time: 97.2 us; the launch traced here: 97 us
  Pallas kernels  96.2 us (99%)
    pallas_call x1, Pallas kernels, layer_call(): pl.pallas_call(functools.partial(layer_kernel, dims), out_shape=[S((T, D)...  89.8 us
    pallas_call x1, Pallas kernels, adam_call(): pl.pallas_call(functools.partial(adam_kernel, n), out_shape=[S(out.shape,...  6.38 us

profile of v3, /device:TPU:0, one launch (start us, length us, event | category | flops | bytes accessed | tf_op | source)
XLA Modules:
  0.0 97.0 jit_solution(8050959757134514880)
XLA Ops:
  0.7 89.8 %layer.1 = (bf16[2048,384]{1,0:T(8,128)(2,1)}, f32[2048,384]{1,0:T(8,128)}, f32[3,16,384]{2,1,0:T(8,128)}, f32[3,16,896]{2,1,0:T(8,128)}, f32[16,384]{1,0:T(8,128)}, /*index=5*/f32[8,128]{1,0:T(8,128)}) custom-call(bf16[2048,384]{1,0:T(8,128)(2,1)} %refs_0_.1, bf16[2048,384]{1,0:T(8,128)(2,1)} %refs_1_.1, s32[32,64,64]{2,1,0:T(8,128)} %refs_2_.1, ...), custom_call_target="tpu_custom_call" | custom-call | tf_op jit(solution)/shard_map/layer/pallas_call | solution.py:660
  90.5 6.4 %adam.1 = (bf16[2048,384]{1,0:T(8,128)(2,1)}, f32[2048,384]{1,0:T(8,128)}, f32[1,1]{1,0:T(1,128)}, f32[12,1152]{1,0:T(8,128)}, f32[12,1152]{1,0:T(8,128)}, /*ind...) custom-call(f32[16,384]{1,0:T(8,128)} %get-tuple-element.42.refs_0_,, ...), custom_call_target="tpu_custom_call" | custom-call | tf_op jit(solution)/shard_map/adam/pallas_call | solution.py:756

commit v4 on v3

--- a/solution.py
+++ b/solution.py
@@ -20,7 +20,6 @@
 RATES = (0.1, 0.5, 0.1, 0.05)
 VECTOR_RATE = 1.0
 TB = 512
-TA = 1024
 TM = 1024
 CH = 256
 
@@ -68,7 +67,7 @@
     return jnp.where(left, r[0:64], r[64:128])
 
 
-def attention_forward(i, g, mask, qkv, probs, mixed):
+def attention_forward(TA, i, g, mask, qkv, probs, mixed):
     left = lane_left()
     across = slice(128 * g, 128 * g + 128)
     clouds = TA // 64
@@ -90,7 +89,7 @@
         mixed[r, across] = diagonal(dot(held[c], v, TN), left).astype(bf16)
 
 
-def attention_backward(i, g, qkv, probs, dmix, dqkv):
+def attention_backward(TA, i, g, qkv, probs, dmix, dqkv):
     left = lane_left()
     across = slice(128 * g, 128 * g + 128)
     rows = [pl.ds(pl.multiple_of(i * TA + 64 * c, 64), 64) for c in range(TA // 64)]
@@ -151,32 +150,29 @@
     def take(count=None):
         return next(it) if count is None else [next(it) for _ in range(count)]
 
-    x_hbm, dy_hbm, mask_hbm, wq_own, wp_own, wu_own, wd_own, vec_own = take(8)
-    out_hbm, ig_hbm, gq_out, gm_out, small_out, norm_out = take(6)
+    x_hbm, dy_hbm, mask_hbm = take(3)
+    own_hbm = take(5)
+    out_hbm, ig_hbm, gq_hbm, gm_hbm, small_out, norm_out = take(6)
+    own = take(5)
+    wq_own, wp_own, wu_own, wd_own, vec_own = own
+    gq_out, gm_out = take(2)
     x, dy, mask, a, qkv, probs, mixed, h1, dh1, c_all, z_all, du_all = take(12)
     bufs = take(NC + 1)
     wq, wp, wu, wd, vec, bu, vgrid, sel, tmp_q = take(9)
     stage = take(NC + 1)
     acc_p, dvec, dbu = take(3)
     r1, r2, r3 = take(NC), take(NC), take(NC)
-    small, s1, s2, s3, sq, sq_in = take(6)
-    local_sem, ag_send, ag_recv, rs_send, rs_recv, ar_send, ar_recv, sq_send, sq_recv = take(9)
+    small, s1, s2, s3, sq, sq_in, far = take(7)
+    local_sem, ag_send, ag_recv, rs_send, rs_recv, ar_send, ar_recv, sq_send, sq_recv, far_send, far_recv = take(11)
     outs = [gq_out.at[k] for k in range(3)] + [gm_out.at[k] for k in range(lay.cuts)]
 
     T = x.shape[0]
     V = vec_own.shape[1]
+    TA = T if n <= 32 else T // 2
     dp = lax.axis_index("dp")
     fs = lax.axis_index("fsdp")
     z, y = dp // Y, lax.rem(dp, Y)
     xx, core = fs // 2, lax.rem(fs, 2)
-
-    loads = [
-        pltpu.make_async_copy(x_hbm, x, local_sem.at[0]),
-        pltpu.make_async_copy(mask_hbm, mask, local_sem.at[1]),
-        pltpu.make_async_copy(dy_hbm, dy, local_sem.at[2]),
-    ]
-    for c in loads:
-        c.start()
 
     chips = [
         (lax.rem(z + k // (X * Y), Z), lax.rem(y + k // X % Y, Y), lax.rem(xx + k % X, X)) for k in range(1, Z * Y * X)
@@ -193,8 +189,21 @@
     for dev in chip_ids + [c_id]:
         pl.semaphore_signal(barrier, inc=1, device_id=dev, device_id_type=MESH)
 
+    own_loads = [pltpu.make_async_copy(a, b, local_sem.at[5 + k]) for k, (a, b) in enumerate(zip(own_hbm, own))]
+    for c in own_loads:
+        c.start()
+    loads = [
+        pltpu.make_async_copy(x_hbm, x, local_sem.at[0]),
+        pltpu.make_async_copy(mask_hbm, mask, local_sem.at[1]),
+        pltpu.make_async_copy(dy_hbm, dy, local_sem.at[2]),
+    ]
+    for c in loads:
+        c.start()
+
     for t in stage:
         t[...] = jnp.zeros_like(t)
+    for k in (0, 1, 4):
+        own_loads[k].wait()
     for g in range(3):
         for j in range(3):
             stage[g][0:R, 128 * j : 128 * j + 128] = wq_own[:, D * j + 128 * g : D * j + 128 * g + 128]
@@ -244,6 +253,24 @@
         return [
             remote(g.at[z_peers[j][0], y, xx, core], r3[ch].at[j], send.at[j], recv.at[j], z_ids[j]) for j in range(P1)
         ]
+
+    def straight(ch):
+        return [
+            remote(bufs[ch].at[c[0], c[1], c[2], core], far.at[k], far_send.at[k], far_recv.at[k], chip_ids[k])
+            for k, c in enumerate(chips)
+        ]
+
+    def straight_step(ch, stage):
+        if stage == 0:
+            for c in straight(ch):
+                c.start()
+        else:
+            for c in straight(ch):
+                c.wait()
+            t = bufs[ch][z, y, xx, core].astype(f32)
+            for k in range(len(chips)):
+                t = t + far[k].astype(f32)
+            outs[ch][...] = t
 
     def scatter_step(ch, stage):
         g = bufs[ch]
@@ -268,7 +295,9 @@
             for j in range(P1):
                 t = t + r3[ch][j].astype(f32)
             outs[ch][...] = t
-        if stage < 3:
+        if ch == 2 and stage == 1:
+            straight_step(ch, 0)
+        elif stage < 3:
             for c in scatter(ch, stage):
                 c.start()
 
@@ -323,6 +352,8 @@
 
     for ch in (VEC, 0, 1, 2):
         gather_step(ch, 0)
+    for k in (2, 3):
+        own_loads[k].wait()
     if lay.straight:
         for nat, _, k, at in lay.pieces:
             stage[3 + k][0:R, at : at + 16] = wu_own[:, nat : nat + 16]
@@ -379,20 +410,15 @@
 
     def pair_forward(g):
         gather_step(g, 3)
+        if g < 2:
+            gather_step(g + 1, 2)
+        if g + 1 < len(MLP):
+            gather_step(MLP[g + 1], 1)
         mine = slice(D * g, D * g + D)
         unpack(wq, mine, [(bufs[g], every, D, 0, 1, 0, None)])
 
         @pl.loop(0, T // TA)
         def _(i):
-            @pl.when(i == 1)
-            def _():
-                if g < 2:
-                    gather_step(g + 1, 2)
-                    if len(MLP) > g + 1:
-                        gather_step(MLP[g + 1], 1)
-                else:
-                    gather_step(MLP[0], 2)
-
             rows = pl.ds(pl.multiple_of(i * TA, TA), TA)
             if g == 0:
                 av = (h1[rows, :] * vec[0:1] + vec[1:2]).astype(bf16)
@@ -400,10 +426,11 @@
             else:
                 av = a[rows, :]
             qkv[rows, mine] = dot(av, wq[:, mine]).astype(bf16)
-            attention_forward(i, g, mask, qkv, probs, mixed)
+            attention_forward(TA, i, g, mask, qkv, probs, mixed)
 
     for g in range(3):
         pair_forward(g)
+    gather_step(MLP[0], 2)
     unpack(wp, every, [(bufs[k], every, D, R, 3, k, None) for k in range(3)])
     if lay.straight:
         for nat, place, _, _ in lay.pieces:
@@ -415,11 +442,6 @@
 
     @pl.loop(0, T // TB)
     def _(i):
-        @pl.when(i == 2)
-        def _():
-            if len(MLP) > 1:
-                gather_step(MLP[1], 2)
-
         rows = pl.ds(pl.multiple_of(i * TB, TB), TB)
         h = x[rows, :].astype(f32) + (dot(mixed[rows, :], wp[...]) + vec[4:5])
         h1[rows, :] = h
@@ -442,8 +464,8 @@
         def _(i):
             @pl.when(i == 1)
             def _():
-                if k == 0 and lay.cuts > 2:
-                    gather_step(MLP[2], 2)
+                if k + 1 < lay.cuts:
+                    gather_step(MLP[k + 1], 2)
                 if k > 0:
                     scatter_step(ch - 1, 1)
 
@@ -475,14 +497,8 @@
 
     dmix = mixed
 
-    @pl.loop(0, T // TM)
+    @pl.loop(0, 2)
     def _(i):
-        @pl.when(i == 1)
-        def _():
-            scatter_step(MLP[-1], 1)
-            if len(MLP) > 1:
-                scatter_step(MLP[0], 2)
-
         rows = pl.ds(pl.multiple_of(i * TM, TM), TM)
         dc = dot(du_all[rows, :], wu[...], NT)
         centered, rstd = ln_parts(h1[rows, :])
@@ -496,6 +512,9 @@
         acc_p[...] += dot(mixed[rows, :], dr, TN)
         dmix[rows, :] = dot(dr, wp[...], NT).astype(bf16)
 
+    scatter_step(MLP[-1], 1)
+    if len(MLP) > 1:
+        scatter_step(MLP[0], 2)
     wp[...] = acc_p[...].astype(bf16)
 
     small[0] = jnp.zeros((16, D), f32)
@@ -537,9 +556,9 @@
     dqkv = du_all
 
     def pair_backward(g):
-        @pl.loop(0, T // TA)
+        @pl.loop(0, 2)
         def _(i):
-            attention_backward(i, g, qkv, probs, dmix, dqkv)
+            attention_backward(T // 2, i, g, qkv, probs, dmix, dqkv)
 
         if g == 0 and len(MLP) > 2:
             scatter_step(MLP[1], 2)
@@ -590,10 +609,6 @@
             scatter_step(MLP[-1], 3)
             scatter_step(0, 3)
 
-        @pl.when(i == 2)
-        def _():
-            scatter_step(2, 2)
-
         rows = pl.ds(pl.multiple_of(i * TB, TB), TB)
         dy[rows, :] = (h1[rows, :] + (dot(z_all[rows, :], wd[...]) + vec[5:6])).astype(bf16)
 
@@ -602,9 +617,15 @@
 
     squares = jnp.zeros((1, 1), f32)
     spread_step(3)
+    put_gm = pltpu.make_async_copy(gm_out, gm_hbm, local_sem.at[10])
+    put_gm.start()
     for ch in MLP + [0, 1, 2]:
-        if ch in (1, 2):
+        if ch == 1:
             scatter_step(ch, 3)
+        if ch == 2:
+            straight_step(ch, 1)
+            put_gq = pltpu.make_async_copy(gq_out, gq_hbm, local_sem.at[11])
+            put_gq.start()
         t = outs[ch][...]
         squares = squares + jnp.sum(jnp.sum(t * t, axis=0, keepdims=True), axis=1, keepdims=True)
     for j in range(6):
@@ -625,8 +646,8 @@
     norm_out[...] = total
     for j in range(6):
         small_out[j // 3 : j // 3 + 1, 128 * (j % 3) : 128 * (j % 3) + 128] = total[j : j + 1]
-    put_out.wait()
-    put_ig.wait()
+    for c in (put_out, put_ig, put_gm, put_gq):
+        c.wait()
 
 
 def layer_call(dims, x, dy, masks, wq, wp, wu, wd, vec):
@@ -643,7 +664,8 @@
     peers = P1 + P2 + 1
     blocks, NC = lay.blocks, lay.chunks
     one_group = n <= 32
-    scratch = [V((T, D), bf16), V((T, D), bf16), V(masks.shape, jnp.int32), V((T, D), bf16), V((T, 3 * D), bf16)]
+    scratch = [V(w.shape, f32) for w in (wq, wp, wu, wd, vec)] + [V((3,) + blocks[0], f32), V((lay.cuts,) + blocks[3], f32)]
+    scratch += [V((T, D), bf16), V((T, D), bf16), V(masks.shape, jnp.int32), V((T, D), bf16), V((T, 3 * D), bf16)]
     scratch += [V((T, D), f32), V((T, D), bf16), V((T, D), f32), V((T, D), f32), V((T, D), bf16)]
     scratch += [V((T, FF), bf16), V((T, FF), bf16)]
     scratch += [V((Z, Y, X, 2) + b, bf16) for b in blocks + ((16, 128),)]
@@ -655,16 +677,16 @@
     scratch += [V((P2, Z) + b, bf16) for b in blocks]
     scratch += [V((P1,) + b, bf16) for b in blocks]
     scratch += [V((3, 16, D), f32), V((P1, 16, D), f32), V((P2, 16, D), f32), V((1, 16, D), f32)]
-    scratch += [V((2, 8, 128), f32), V((chips + 1, 8, 128), f32)]
-    scratch += [dma((5,))] + [dma((NC + 1, peers))] * 4 + [dma((peers,))] * 2 + [dma((chips + 1,))] * 2
+    scratch += [V((2, 8, 128), f32), V((chips + 1, 8, 128), f32), V((chips,) + blocks[0], bf16)]
+    scratch += [dma((20,))] + [dma((NC + 1, peers))] * 4 + [dma((peers,))] * 2 + [dma((chips + 1,))] * 2 + [dma((chips,))] * 2
     return pl.pallas_call(
         functools.partial(layer_kernel, dims),
         out_shape=[
             S((T, D), bf16), S((T, D), f32), S((3,) + blocks[0], f32), S((lay.cuts,) + blocks[3], f32),
             S((16, D), f32), S((8, 128), f32),
         ],
-        in_specs=[hbm] * 3 + [vm] * 5,
-        out_specs=[hbm] * 2 + [vm] * 4,
+        in_specs=[hbm] * 8,
+        out_specs=[hbm] * 4 + [vm] * 2,
         scratch_shapes=scratch,
         compiler_params=pltpu.CompilerParams(
             collective_id=0, has_side_effects=True, vmem_limit_bytes=62 * 1024 * 1024
@@ -682,43 +704,56 @@
 
 
 def adam_kernel(n, *refs):
-    small, matrix_squares, gq, gm = refs[0:4]
-    state = refs[4:19]
+    small_in, norm_in, gq_in, gm_in = refs[0:4]
+    state_in = refs[4:19]
     out_in, ig_in = refs[19:21]
     out_ref, ig_ref, norm = refs[21:24]
     new_hbm = refs[24:39]
-    sem, out_v, ig_v, up = refs[39:43]
-    new = refs[43:58]
+    sem, small, matrix_squares, gq, gm, out_v, ig_v, up = refs[39:47]
+    state, new = refs[47:62], refs[62:77]
     lay = Layout(n)
     R, Rd, V = lay.R, lay.Rd, state[12].shape[1]
     T = out_v.shape[0]
-    pieces = 4
-    parts = [pl.ds(k * (T // pieces), T // pieces) for k in range(pieces)]
-    moves = [(a, b, c, r) for r in parts for a, b, c in ((ig_in, ig_v, ig_ref), (out_in, out_v, out_ref))]
-    loads = [pltpu.make_async_copy(a.at[r], b.at[r], sem.at[k]) for k, (a, b, c, r) in enumerate(moves)]
-    stores = [pltpu.make_async_copy(b.at[r], c.at[r], sem.at[k + len(moves)]) for k, (a, b, c, r) in enumerate(moves)]
-    for c in loads:
+    sems = iter(range(sem.shape[0]))
+
+    def copy(a, b):
+        return pltpu.make_async_copy(a, b, sem.at[next(sems)])
+
+    first = [copy(a, b) for a, b in ((small_in, small), (norm_in, matrix_squares), (gm_in, gm), (gq_in, gq))]
+    gets = [copy(a, b) for a, b in zip(state_in, state)]
+    puts = [copy(a, b) for a, b in zip(new, new_hbm)]
+    pieces = [pl.ds(k * (T // 4), T // 4) for k in range(4)]
+    moves = [(a.at[r], b.at[r], c.at[r]) for r in pieces for a, b, c in ((ig_in, ig_v, ig_ref), (out_in, out_v, out_ref))]
+    loads = [copy(a, b) for a, b, _ in moves]
+    stores = [copy(b, c) for _, b, c in moves]
+    order = (2, 3, 0, 1, 4)
+    for c in first + [gets[3 * k + j] for k in order[:2] for j in range(3)] + loads[:2]:
         c.start()
-    puts = [pltpu.make_async_copy(a, b, sem.at[2 * len(moves) + k]) for k, (a, b) in enumerate(zip(new, new_hbm))]
+    for c in [gets[3 * k + j] for k in order[2:] for j in range(3)] + loads[2:]:
+        c.start()
+
+    def pass_on(lo, hi):
+        for c, d in zip(loads[lo:hi], stores[lo:hi]):
+            c.wait()
+            d.start()
+
+    for c in first:
+        c.wait()
     vecs = small[0:10]
     squares = jnp.sum(jnp.sum(vecs * vecs, axis=0, keepdims=True), axis=1, keepdims=True) + matrix_squares[6:7, 0:1]
     clip = jnp.sqrt(squares)
     norm[...] = clip
     factor = 1.0 / clip
 
-    def step(k, rows, cols, g, rate, decay):
-        w, m, r = (ref[rows, cols] for ref in state[3 * k : 3 * k + 3])
+    def step(k, g, rate, decay):
+        for c in gets[3 * k : 3 * k + 3]:
+            c.wait()
+        w, m, r = (ref[...] for ref in state[3 * k : 3 * k + 3])
         for ref, value in zip(new[3 * k : 3 * k + 3], adam_step(w, m, r, g * factor, rate, decay)):
-            ref[rows, cols] = value
-
-    def put(k):
+            ref[...] = value
         for c in puts[3 * k : 3 * k + 3]:
             c.start()
 
-    for c, d in zip(loads, stores):
-        c.wait()
-        d.start()
-    every = slice(0, D)
     if lay.straight:
         for nat, _, k, at in lay.pieces:
             up[:, nat : nat + 16] = gm[k, 0:R, at : at + 16]
@@ -727,23 +762,22 @@
         for k in range(FF // D):
             up[:, D * k : D * k + D] = gm[0, R * k : R * k + R, 0:D]
         down = gm[0, 0:Rd, D : 2 * D]
-    step(2, slice(0, R), slice(0, FF), up[...], RATES[2], DECAY)
-    put(2)
-    step(3, slice(0, Rd), every, down, RATES[3], DECAY)
-    put(3)
+    pass_on(0, 2)
+    step(2, up[...], RATES[2], DECAY)
+    pass_on(2, 4)
+    step(3, down, RATES[3], DECAY)
+    pass_on(4, 6)
     g = jnp.concatenate([gq[k, 0:R, 128 * j : 128 * j + 128] for j in range(3) for k in range(3)], axis=1)
-    step(0, slice(0, R), slice(0, 3 * D), g, RATES[0], DECAY)
-    put(0)
+    step(0, g, RATES[0], DECAY)
+    pass_on(6, 8)
     g = jnp.concatenate([gq[i % 3, R + i // 3 : R + i // 3 + 1] for i in range(R)], axis=0)
-    step(1, slice(0, R), every, g, RATES[1], DECAY)
-    put(1)
+    step(1, g, RATES[1], DECAY)
     me = lax.axis_index("dp") * (n // lax.axis_size("dp")) + lax.axis_index("fsdp")
     start = me * V
     row, lane = start // D, lax.rem(start, D)
     two = jnp.concatenate([small[pl.ds(row, 1), :], small[pl.ds(row + 1, 1), :]], axis=1)
     two = pltpu.roll(jnp.broadcast_to(two, (8, 2 * D)), 2 * D - lane, 1)
-    step(4, slice(0, 1), slice(0, V), two[0:1, 0:V], VECTOR_RATE, 0.0)
-    put(4)
+    step(4, two[0:1, 0:V], VECTOR_RATE, 0.0)
     for c in stores + puts:
         c.wait()
 
@@ -753,14 +787,14 @@
     hbm = pl.BlockSpec(memory_space=pl.ANY)
     S = jax.ShapeDtypeStruct
     V = pltpu.VMEM
+    held = [V(v.shape, v.dtype) for v in (small, squares, gq, gm, out, ig)] + [V((D // n, FF), f32)]
     return pl.pallas_call(
         functools.partial(adam_kernel, n),
         out_shape=[S(out.shape, out.dtype), S(ig.shape, ig.dtype), S((1, 1), f32)] + [S(s.shape, f32) for s in state],
-        in_specs=[vm] * 19 + [hbm] * 2,
+        in_specs=[hbm] * 21,
         out_specs=[hbm] * 2 + [vm] + [hbm] * 15,
-        scratch_shapes=[pltpu.SemaphoreType.DMA((31,)), V(out.shape, out.dtype), V(ig.shape, ig.dtype)]
-        + [V((D // n, FF), f32)]
-        + [V(s.shape, f32) for s in state],
+        scratch_shapes=[pltpu.SemaphoreType.DMA((50,))] + held + [V(s.shape, f32) for s in state] * 2,
+        compiler_params=pltpu.CompilerParams(vmem_limit_bytes=62 * 1024 * 1024),
         name="adam",
     )(small, squares, gq, gm, *state, out, ig)
 

time: 97.2 us -> 94.5 us (0.972)
  Pallas kernels: 96.2 us -> 93.5 us
    pallas_call x1, Pallas kernels: 89.8 us -> 88 us  [layer_call(): pl.pallas_call(functools.partial(layer_kernel, dims), out_shape=[S((T, D)...]
where the time goes in v4:
time: 94.5 us; the launch traced here: 94.3 us
  Pallas kernels  93.5 us (99%)
    pallas_call x1, Pallas kernels, layer_call(): pl.pallas_call(functools.partial(layer_kernel, dims), out_shape=[S((T, D)...  88 us
    pallas_call x1, Pallas kernels, adam_call(): pl.pallas_call(functools.partial(adam_kernel, n), out_shape=[S(out.shape,...  5.45 us

profile of v4, /device:TPU:0, one launch (start us, length us, event | category | flops | bytes accessed | tf_op | source)
XLA Modules:
  0.0 94.3 jit_solution(10454354905953941762)
XLA Ops:
  0.7 88.0 %layer.1 = (bf16[2048,384]{1,0:T(8,128)(2,1)}, f32[2048,384]{1,0:T(8,128)}, f32[3,16,384]{2,1,0:T(8,128)}, f32[3,16,896]{2,1,0:T(8,128)}, f32[16,384]{1,0:T(8,128)}, /*index=5*/f32[8,128]{1,0:T(8,128)}) custom-call(bf16[2048,384]{1,0:T(8,128)(2,1)} %refs_0_.1, bf16[2048,384]{1,0:T(8,128)(2,1)} %refs_1_.1, s32[32,64,64]{2,1,0:T(8,128)} %refs_2_.1, ...), custom_call_target="tpu_custom_call" | custom-call | tf_op jit(solution)/shard_map/layer/pallas_call | solution.py:682
  88.7 5.5 %adam.1 = (bf16[2048,384]{1,0:T(8,128)(2,1)}, f32[2048,384]{1,0:T(8,128)}, f32[1,1]{1,0:T(1,128)}, f32[12,1152]{1,0:T(8,128)}, f32[12,1152]{1,0:T(8,128)}, /*ind...) custom-call(f32[16,384]{1,0:T(8,128)} %get-tuple-element.42.refs_0_,, ...), custom_call_target="tpu_custom_call" | custom-call | tf_op jit(solution)/shard_map/adam/pallas_call | solution.py:791

commit v5 on v4

--- a/solution.py
+++ b/solution.py
@@ -212,8 +212,6 @@
     stage[VEC][0:1, 0:V] = vec_own[...]
     for ch in (0, 1, 2, VEC):
         bufs[ch][z, y, xx, core] = stage[ch][...].astype(bf16)
-
-    pl.semaphore_wait(barrier, len(chip_ids) + 1)
 
     def remote(src, dst, send, recv, dev):
         return pltpu.make_async_remote_copy(
@@ -350,6 +348,28 @@
 
     every = slice(0, D)
 
+    if n_groups == 1:
+        for (shift, step, first), k in SEL.items():
+            sel[k] = pick_rows((0, n, n), D, shift, step, first)
+    for r in (acc_p, dvec, dbu):
+        r[...] = jnp.zeros_like(r)
+    for c in loads:
+        c.wait()
+
+    @pl.loop(0, T // TB)
+    def _(i):
+        rows = pl.ds(pl.multiple_of(i * TB, TB), TB)
+        centered, rstd = ln_parts(x[rows, :].astype(f32))
+        h1[rows, :] = centered * rstd
+        key = lax.broadcasted_iota(jnp.int32, (64, 64), 0)
+        query = lax.broadcasted_iota(jnp.int32, (64, 64), 1)
+        clouds = TB // 64
+        for c in range(clouds):
+            allowed = (key <= query) & ((mask[i * clouds + c].T == 1) | (key == query))
+            mask[i * clouds + c] = jnp.where(allowed, 1, 0)
+
+    pl.semaphore_wait(barrier, len(chip_ids) + 1)
+
     for ch in (VEC, 0, 1, 2):
         gather_step(ch, 0)
     for k in (2, 3):
@@ -366,26 +386,6 @@
     for ch in MLP:
         bufs[ch][z, y, xx, core] = stage[ch][...].astype(bf16)
         gather_step(ch, 0)
-    if n_groups == 1:
-        for (shift, step, first), k in SEL.items():
-            sel[k] = pick_rows((0, n, n), D, shift, step, first)
-    for r in (acc_p, dvec, dbu):
-        r[...] = jnp.zeros_like(r)
-    for c in loads:
-        c.wait()
-
-    @pl.loop(0, T // TB)
-    def _(i):
-        rows = pl.ds(pl.multiple_of(i * TB, TB), TB)
-        centered, rstd = ln_parts(x[rows, :].astype(f32))
-        h1[rows, :] = centered * rstd
-        key = lax.broadcasted_iota(jnp.int32, (64, 64), 0)
-        query = lax.broadcasted_iota(jnp.int32, (64, 64), 1)
-        clouds = TB // 64
-        for c in range(clouds):
-            allowed = (key <= query) & ((mask[i * clouds + c].T == 1) | (key == query))
-            mask[i * clouds + c] = jnp.where(allowed, 1, 0)
-
     for ch in (VEC, 0, 1, 2):
         gather_step(ch, 1)
     gather_step(MLP[0], 1)
@@ -408,6 +408,14 @@
             vec[r0 : r0 + 1, l0 : l0 + size] = vgrid[d : d + 1, o : o + size]
             start += size
 
+    if lay.straight:
+        for nat, place, _, _ in lay.pieces:
+            r0, l0 = 6 + nat // D, nat % D
+            bu[:, place : place + 16] = vec[r0 : r0 + 1, l0 : l0 + 16]
+    else:
+        for k in range(FF // D):
+            bu[:, D * k : D * k + D] = vec[6 + k : 7 + k]
+
     def pair_forward(g):
         gather_step(g, 3)
         if g < 2:
@@ -432,14 +440,6 @@
         pair_forward(g)
     gather_step(MLP[0], 2)
     unpack(wp, every, [(bufs[k], every, D, R, 3, k, None) for k in range(3)])
-    if lay.straight:
-        for nat, place, _, _ in lay.pieces:
-            r0, l0 = 6 + nat // D, nat % D
-            bu[:, place : place + 16] = vec[r0 : r0 + 1, l0 : l0 + 16]
-    else:
-        for k in range(FF // D):
-            bu[:, D * k : D * k + D] = vec[6 + k : 7 + k]
-
     @pl.loop(0, T // TB)
     def _(i):
         rows = pl.ds(pl.multiple_of(i * TB, TB), TB)
@@ -722,14 +722,12 @@
     first = [copy(a, b) for a, b in ((small_in, small), (norm_in, matrix_squares), (gm_in, gm), (gq_in, gq))]
     gets = [copy(a, b) for a, b in zip(state_in, state)]
     puts = [copy(a, b) for a, b in zip(new, new_hbm)]
-    pieces = [pl.ds(k * (T // 4), T // 4) for k in range(4)]
+    pieces = [pl.ds(k * (T // 2), T // 2) for k in range(2)]
     moves = [(a.at[r], b.at[r], c.at[r]) for r in pieces for a, b, c in ((ig_in, ig_v, ig_ref), (out_in, out_v, out_ref))]
     loads = [copy(a, b) for a, b, _ in moves]
     stores = [copy(b, c) for _, b, c in moves]
     order = (2, 3, 0, 1, 4)
-    for c in first + [gets[3 * k + j] for k in order[:2] for j in range(3)] + loads[:2]:
-        c.start()
-    for c in [gets[3 * k + j] for k in order[2:] for j in range(3)] + loads[2:]:
+    for c in first + [gets[3 * k + j] for k in order for j in range(3)] + loads:
         c.start()
 
     def pass_on(lo, hi):
@@ -762,14 +760,14 @@
         for k in range(FF // D):
             up[:, D * k : D * k + D] = gm[0, R * k : R * k + R, 0:D]
         down = gm[0, 0:Rd, D : 2 * D]
-    pass_on(0, 2)
+    pass_on(0, 1)
     step(2, up[...], RATES[2], DECAY)
-    pass_on(2, 4)
+    pass_on(1, 2)
     step(3, down, RATES[3], DECAY)
-    pass_on(4, 6)
+    pass_on(2, 3)
     g = jnp.concatenate([gq[k, 0:R, 128 * j : 128 * j + 128] for j in range(3) for k in range(3)], axis=1)
     step(0, g, RATES[0], DECAY)
-    pass_on(6, 8)
+    pass_on(3, 4)
     g = jnp.concatenate([gq[i % 3, R + i // 3 : R + i // 3 + 1] for i in range(R)], axis=0)
     step(1, g, RATES[1], DECAY)
     me = lax.axis_index("dp") * (n // lax.axis_size("dp")) + lax.axis_index("fsdp")

time: 94.5 us -> 96.8 us (1.024)
  Pallas kernels: 93.5 us -> 95.7 us
    pallas_call x1, Pallas kernels: 88 us -> 90.4 us  [layer_call(): pl.pallas_call(functools.partial(layer_kernel, dims), out_shape=[S((T, D)...]
where the time goes in v5:
time: 96.8 us; the launch traced here: 96.6 us
  Pallas kernels  95.7 us (99%)
    pallas_call x1, Pallas kernels, layer_call(): pl.pallas_call(functools.partial(layer_kernel, dims), out_shape=[S((T, D)...  90.4 us
    pallas_call x1, Pallas kernels, adam_call(): pl.pallas_call(functools.partial(adam_kernel, n), out_shape=[S(out.shape,...  5.37 us

profile of v5, /device:TPU:0, one launch (start us, length us, event | category | flops | bytes accessed | tf_op | source)
XLA Modules:
  0.0 96.6 jit_solution(15021571460039164733)
XLA Ops:
  0.7 90.4 %layer.1 = (bf16[2048,384]{1,0:T(8,128)(2,1)}, f32[2048,384]{1,0:T(8,128)}, f32[3,16,384]{2,1,0:T(8,128)}, f32[3,16,896]{2,1,0:T(8,128)}, f32[16,384]{1,0:T(8,128)}, /*index=5*/f32[8,128]{1,0:T(8,128)}) custom-call(bf16[2048,384]{1,0:T(8,128)(2,1)} %refs_0_.1, bf16[2048,384]{1,0:T(8,128)(2,1)} %refs_1_.1, s32[32,64,64]{2,1,0:T(8,128)} %refs_2_.1, ...), custom_call_target="tpu_custom_call" | custom-call | tf_op jit(solution)/shard_map/layer/pallas_call | solution.py:682
  91.0 5.4 %adam.1 = (bf16[2048,384]{1,0:T(8,128)(2,1)}, f32[2048,384]{1,0:T(8,128)}, f32[1,1]{1,0:T(1,128)}, f32[12,1152]{1,0:T(8,128)}, f32[12,1152]{1,0:T(8,128)}, /*ind...) custom-call(f32[16,384]{1,0:T(8,128)} %get-tuple-element.42.refs_0_,, ...), custom_call_target="tpu_custom_call" | custom-call | tf_op jit(solution)/shard_map/adam/pallas_call | solution.py:789
